TPU v7x, 128 devices: a whole 4x4x4 slice. The times are simulated.
128 devices in a mesh: row: 8 (over x, y_lo), col: 16 (over y_hi, z, core).
Axes of the slice: x: 4, y: 4 (y_hi: 2, y_lo: 2; y = y_hi * 2 + y_lo), z: 4, core: 2. Of those that a mesh axis runs over, the one named last changes fastest.
Arguments:
- front: float32 [10240, 10240], P('row', 'col'), as said below
- updates: float32 [16384, 8192], P('row', 'col'), as said below
- maps: int32 [2, 64], replicated, may hold values from 0 to 79, as said below
Outputs:
- panel_factor: float32 [10240, 2048], P('row', 'col')
- trailing: float32 [10240, 10240], P('row', 'col')
Inputs may be any that keep to these rules, and one draw needn't show every extreme that they name: `maps`: each row lists 64 distinct front blocks; entry j leaves remainder floor(j / 4) on division by 16, the entries of one remainder rise with j, and blocks 0 and 79 appear in both rows. Symmetric in front order; the assembled leading 2048 x 2048 block is positive definite. `updates`: each child's update is symmetric in the child's own order.
All inputs are finite; a program needn't handle non-finite values.
Results may differ from a plain program's by a relative error of at most 0.0001.
Values sent between devices are 32-bit elements; how exact they have to be, the bound alone decides.
No kernel may reach another device: no remote copies, remote signals or barrier semaphores. Data moves between devices by JAX's collectives and lax.ppermute only.
A program may use at most 192 MiB of HBM per device.

v0:
```python
import functools

import jax
import jax.numpy as jnp
from jax import lax
from jax.experimental import pallas as pl
from jax.experimental.pallas import tpu as pltpu
from jax.sharding import PartitionSpec as P

BLK = 128
PW = 2048
STRIPS = ((0, 1024), (1024, 512), (1536, 512))
STEP = 256
BOTH = ("row", "col")
OFFSETS = (0, -1, 1, 2)
NEAR = 2
F32 = jnp.float32
BF16 = jnp.bfloat16
PARAMS = pltpu.CompilerParams(vmem_limit_bytes=58 << 20)
ANY = pl.BlockSpec(memory_space=pl.ANY)
VMEM = pl.BlockSpec(memory_space=pltpu.VMEM)
SMEM = pl.BlockSpec(memory_space=pltpu.SMEM)


def flat(x, y, z, core):
    return ((x % 4) * 2 + y % 2) * 16 + ((y % 4) // 2) * 8 + (z % 4) * 2 + core % 2


def move(value, *by):
    every = [(x, y, z, c) for x in range(4) for y in range(4) for z in range(4) for c in range(2)]
    pairs = []
    for x, y, z, c in every:
        step = by[c] if len(by) > 1 else by[0]
        if step is not None:
            pairs.append((flat(x, y, z, c), flat(x + step[0], y + step[1], z + step[2], c + step[3])))
    return lax.ppermute(value, BOTH, pairs)


SWAP = (0, 0, 0, 1)


def around(value, *axes):
    out = [value]
    for offset in OFFSETS[1:]:
        out.append(move(value, *[tuple(-offset if n == axis else 0 for n in range(4)) for axis in axes]))
    return out


def settled(value, *tokens):
    ready = functools.reduce(jnp.logical_and, [token <= F32(jnp.finfo(jnp.float32).max) for token in tokens])
    return jnp.where(ready, value, jnp.zeros((), value.dtype))


def gather_leading(corner, y_at, core_at):
    first = core_at == 0
    upper, lower = corner[:BLK], corner[BLK:]
    mine = jnp.where(first, upper, lower)
    other = move(jnp.where(first, lower, upper), SWAP)
    both = jnp.stack([jnp.where(first, mine, other), jnp.where(first, other, mine)])
    own, below, above, opposite = around(both, 1)
    blocks = []
    for y in range(4):
        d = (y - y_at) & 3
        blocks.append(jnp.where(d == 0, own, jnp.where(d == 1, above, jnp.where(d == 2, opposite, below))))
    group = jnp.stack(around(jnp.stack(blocks), 2, 0))
    mine = around(group[:, :2], 0, 2)
    pieces = [*mine, *[move(piece, SWAP) for piece in mine]]
    late = jnp.where(first, move(group[:, 2], SWAP), group[:, 3])
    return pieces, late


def eliminate(tiles):
    tiles = list(tiles)
    count = len(tiles)
    lane = lax.broadcasted_iota(jnp.int32, (8, BLK), 1)
    sub = lax.broadcasted_iota(jnp.int32, (8, BLK), 0)
    upper = []

    def by_lane(x, j):
        return jnp.broadcast_to(x[:, j : j + 1], (8, BLK))

    def by_sub(x, s):
        return jnp.broadcast_to(x[s : s + 1, :], (8, BLK))

    for p in range(count):
        now = tiles[p]
        o = 8 * p
        inside = (lane >= o) & (lane < o + 8)
        column = [by_lane(now, o + t) for t in range(8)]
        a = {(s, t): by_sub(column[t], s) for t in range(8) for s in range(t, 8)}
        rows = [by_sub(now, t) for t in range(8)]
        unit = [jnp.where(lane == o + t, F32(1), jnp.where(inside, F32(0), rows[t])) for t in range(8)]
        r = []
        low = {}
        for t in range(8):
            r.append(lax.rsqrt(a[t, t]))
            for s in range(t + 1, 8):
                low[s, t] = a[s, t] * r[t]
            for u in range(t + 1, 8):
                for s in range(u, 8):
                    a[s, u] = a[s, u] - low[s, t] * low[u, t]
        z = []
        q = []
        for t in range(8):
            z_now, q_now = unit[t], rows[t]
            for s in range(t):
                z_now = z_now - low[t, s] * z[s]
                q_now = q_now - low[t, s] * q[s]
            z.append(z_now * r[t])
            q.append(q_now * r[t])
        y = [None] * 8
        for t in reversed(range(8)):
            y_now = z[t]
            for s in range(t + 1, 8):
                y_now = y_now - low[s, t] * y[s]
            y[t] = y_now * r[t]
        z_tile, q_tile, y_tile = z[0], q[0], y[0]
        for t in range(1, 8):
            z_tile = jnp.where(sub == t, z[t], z_tile)
            q_tile = jnp.where(sub == t, q[t], q_tile)
            y_tile = jnp.where(sub == t, y[t], y_tile)
        upper.append(jnp.where(lane >= o + sub, q_tile, F32(0)))
        tiles[p] = jnp.where(lane <= o + sub, z_tile, F32(0))
        for i in range(p + 1, min(p + 1 + NEAR, count)):
            terms = [by_lane(tiles[i], o + t) * y[t] for t in range(8)]
            while len(terms) > 1:
                terms = [terms[k] + terms[k + 1] for k in range(0, len(terms), 2)]
            tiles[i] = jnp.where(inside, F32(0), tiles[i]) - terms[0]
        far = p + 1 + NEAR
        if far < count:
            zero = jnp.zeros((8, BLK), F32)
            padded = jnp.concatenate([zero] * p + [y_tile] + [zero] * (count - p - 1), axis=0)
            less = exact_nn(jnp.concatenate(tiles[far:], axis=0), padded)
            for i in range(far, count):
                tiles[i] = jnp.where(inside, F32(0), tiles[i]) - less[8 * (i - far) : 8 * (i - far) + 8]
    return tiles, upper


def split(x):
    high = x.astype(BF16)
    return high, (x - high.astype(F32)).astype(BF16)


def dot_nt(a, b):
    return lax.dot_general(a, b, (((1,), (1,)), ((), ())), preferred_element_type=F32)


def dot_nn(a, b):
    return lax.dot_general(a, b, (((1,), (0,)), ((), ())), preferred_element_type=F32)


def pairs(dot, ah, al, bh, bl):
    return dot(ah, bh) + (dot(ah, bl) + dot(al, bh))


def exact_nt(a, b):
    return lax.dot_general(a, b, (((1,), (1,)), ((), ())), precision=lax.Precision.HIGHEST, preferred_element_type=F32)


def exact_nn(a, b):
    return jnp.dot(a, b, precision=lax.Precision.HIGHEST, preferred_element_type=F32)


def offset_of(index):
    return jnp.where(index == 3, 2, jnp.where(index == 2, 1, jnp.where(index == 1, -1, 0)))


def load_leading(place, pieces, late, dest, sems, first_col):
    x, z, core = place[0], place[2], place[3]
    count = dest.shape[0]

    def fetch(source, block_row, block_col):
        pltpu.make_async_copy(
            source,
            dest.at[block_col, pl.ds(pl.multiple_of(block_row * BLK, BLK), BLK), :],
            sems.at[block_col >> 2],
        ).start()

    if late:
        for swapped, ref in enumerate(pieces):
            low_y = (core + swapped) & 1

            def one(n, carry, ref=ref, low_y=low_y):
                far, near, c = n >> 3, (n >> 1) & 3, n & 1
                block_row = ((x + offset_of(near)) & 3) * 2 + low_y + 8
                block_col = 8 + ((z + offset_of(far)) & 3) * 2 + c - first_col

                @pl.when((block_col >= 0) & (block_col < count))
                def _():
                    fetch(ref.at[far, near, c], block_row, block_col)

                return carry

            lax.fori_loop(0, 32, one, 0)
        return
    for number, ref in enumerate(pieces):
        half = (core + number // 4) & 1
        far = OFFSETS[number % 4]

        def one(n, carry, ref=ref, half=half, far=far):
            i, y, c = n >> 2, (n >> 1) & 1, n & 1
            near = offset_of(i)
            dx, dz = jnp.where(half == 0, far, near), jnp.where(half == 0, near, far)
            fetch(ref.at[i, y, c], ((x + dx) & 3) * 2 + y + 8 * half, ((z + dz) & 3) * 2 + c - first_col)
            return carry

        lax.fori_loop(0, 16, one, 0)


def factor_kernel(call, place, *refs):
    start, width = STRIPS[call]
    late = start >= PW // 2
    count = 2 if late else 8
    pieces, refs = refs[:count], refs[count:]
    earlier = refs[: 2 * call]
    out_high, out_low, inv_high, inv_low = refs[2 * call : 4 + 2 * call]
    (lead, high, low, c, diag, inverse, upper, inverse1, low21, load_sem, strip_sem, out_sem) = refs[4 + 2 * call :]
    load_leading(place, pieces, late, lead, load_sem, start // BLK)
    copies = []
    for n in range(call):
        for which, dest in ((0, high), (1, low)):
            copies.append(
                pltpu.make_async_copy(
                    earlier[2 * n + which].at[pl.ds(start - STRIPS[n][0], PW - start), :],
                    dest.at[:, pl.ds(*STRIPS[n])],
                    strip_sem.at[2 * n + which],
                )
            )
    for copy in copies:
        copy.start()

    def wait_lead(n):
        loaded = lead.at[4 * n : 4 * n + 4, PW // 2 if late else 0 :, :]
        pltpu.make_async_copy(loaded, loaded, load_sem.at[n]).wait()

    def outs(kk):
        rows, cols = pl.ds(STEP * kk, PW - start - STEP * kk), pl.ds(STEP * kk, STEP)
        source = pl.ds(start + STEP * kk, STEP)
        return [
            pltpu.make_async_copy(high.at[rows, source], out_high.at[rows, cols], out_sem.at[2 * kk]),
            pltpu.make_async_copy(low.at[rows, source], out_low.at[rows, cols], out_sem.at[2 * kk + 1]),
        ]

    wait_lead(0)
    for copy in copies:
        copy.wait()

    def put(rows, cols, value):
        h, l = split(value)
        high[rows, cols] = h
        low[rows, cols] = l

    def before(kk):
        if kk and kk % 2 == 0:
            wait_lead(kk // 2)
        known = start + STEP * kk
        r0 = STEP * kk
        tiles = (PW - start - r0) // STEP

        def tile(t, carry):
            at = pl.multiple_of(r0 + t * STEP, STEP)
            rows = pl.ds(at, STEP)
            whole = pl.ds(pl.multiple_of(start + at, STEP), STEP)
            value = jnp.concatenate([lead[2 * kk, whole, :], lead[2 * kk + 1, whole, :]], axis=1)
            if known > 0:
                value = value - pairs(
                    dot_nt, high[rows, :known], low[rows, :known], high[r0 : r0 + STEP, :known], low[r0 : r0 + STEP, :known]
                )
            c[rows, :] = value
            return carry

        lax.fori_loop(0, tiles, tile, 0)
        diag[...] = c[r0 : r0 + BLK, :BLK]

    def between(kk):
        r0 = STEP * kk
        col = start + r0
        w1 = inverse[...]
        l21 = exact_nt(c[r0 + BLK : r0 + STEP, :BLK], w1)
        diag[...] = c[r0 + BLK : r0 + STEP, BLK:] - exact_nt(l21, l21)
        inverse1[...] = w1
        low21[...] = l21
        put(pl.ds(r0, BLK), pl.ds(col, BLK), upper[...].T)
        put(pl.ds(r0, BLK), pl.ds(col + BLK, BLK), jnp.zeros((BLK, BLK), F32))
        put(pl.ds(r0 + BLK, BLK), pl.ds(col, BLK), l21)

    def after(kk):
        r0 = STEP * kk
        col = start + r0
        w2 = inverse[...]
        put(pl.ds(r0 + BLK, BLK), pl.ds(col + BLK, BLK), upper[...].T)
        w21 = -exact_nn(w2, exact_nn(low21[...], inverse1[...]))
        top = jnp.concatenate([inverse1[...], jnp.zeros((BLK, BLK), F32)], axis=1)
        w = jnp.concatenate([top, jnp.concatenate([w21, w2], axis=1)], axis=0)
        wh, wl = split(w)
        inv_high[kk] = wh
        inv_low[kk] = wl
        tiles = (PW - start - r0) // STEP

        def tile(t, carry):
            rows = pl.ds(pl.multiple_of(r0 + t * STEP, STEP), STEP)
            ch, cl = split(c[rows, :])
            put(rows, pl.ds(col, STEP), pairs(dot_nt, ch, cl, inv_high[kk], inv_low[kk]))
            return carry

        lax.fori_loop(1, tiles, tile, 0)
        for copy in outs(kk):
            copy.start()

    def half(h, carry):
        for kk in range(width // STEP):
            pl.when(h == 2 * kk)(functools.partial(before, kk))
        w, u = eliminate([diag[8 * i : 8 * i + 8, :] for i in range(16)])
        for i in range(16):
            inverse[8 * i : 8 * i + 8, :] = w[i]
            upper[8 * i : 8 * i + 8, :] = u[i]
        for kk in range(width // STEP):
            pl.when(h == 2 * kk)(functools.partial(between, kk))
            pl.when(h == 2 * kk + 1)(functools.partial(after, kk))
        return carry

    lax.fori_loop(0, width // BLK, half, 0)
    for kk in range(width // STEP):
        for copy in outs(kk):
            copy.wait()


def factor_strip(call, place, pieces, earlier):
    start, width = STRIPS[call]
    rows = PW - start
    known = start + width
    strip = jax.ShapeDtypeStruct((rows, width), BF16)
    inverses = jax.ShapeDtypeStruct((width // STEP, STEP, STEP), BF16)
    block = pltpu.VMEM((BLK, BLK), F32)
    return pl.pallas_call(
        functools.partial(factor_kernel, call),
        out_shape=[strip, strip, inverses, inverses],
        in_specs=[SMEM] + [ANY] * (len(pieces) + 2 * call),
        out_specs=[ANY, ANY, VMEM, VMEM],
        scratch_shapes=[
            pltpu.VMEM((width // BLK, PW, BLK), F32),
            pltpu.VMEM((rows, known), BF16),
            pltpu.VMEM((rows, known), BF16),
            pltpu.VMEM((rows, STEP), F32),
            block,
            block,
            block,
            block,
            block,
            pltpu.SemaphoreType.DMA((width // 512,)),
            pltpu.SemaphoreType.DMA((max(2 * call, 1),)),
            pltpu.SemaphoreType.DMA((2 * width // STEP,)),
        ],
        compiler_params=PARAMS,
        cost_estimate=pl.CostEstimate(flops=int(7e7) * width, bytes_accessed=int(1e8), transcendentals=0),
        name=f"factor{call}",
    )(place, *pieces, *earlier)


def solve_kernel(place, source, colsel, *refs):
    n_strips = 2 * len(STRIPS)
    strips, inverses, refs = refs[:n_strips], refs[n_strips : 2 * n_strips], refs[2 * n_strips :]
    slabs, refs = refs[:8], refs[8:]
    panel_rows, front, first, rest, panel_out, trailing = refs[:6]
    high, low, xh, xl, yh, yl, raw, yraw, base, child, sems, raw_sem, slab_sem, child_sem = refs[6:]
    x, y, z, core = place[0], place[1], place[2], place[3]
    row = x * 2 + y % 2
    col = (y // 2) * 8 + z * 2 + core
    wait_strip = {}
    for n, (start, width) in enumerate(STRIPS):
        rows, cols = pl.ds(start, PW - start), pl.ds(start, width)
        wait_strip[start] = [
            pltpu.make_async_copy(strips[2 * n + which], dest.at[rows, cols], sems.at[2 * n + which])
            for which, dest in ((0, high), (1, low))
        ]
    raws = [pltpu.make_async_copy(panel_rows.at[pl.ds(4 * n, 4)], raw.at[pl.ds(4 * n, 4)], raw_sem.at[n]) for n in range(4)]
    slab_copies = []
    for dx in range(4):
        for dl in range(2):
            there = ((x + dx) % 4) * 2 + (y + dl) % 2
            for second in range(2):
                at = pl.multiple_of((there + 8 * second) * BLK, BLK)
                slab_copies.append(
                    pltpu.make_async_copy(
                        slabs[dx * 2 + dl].at[pl.ds(second * BLK, BLK), :],
                        yraw.at[pl.ds(at, BLK), :],
                        slab_sem.at[(dx * 2 + dl) * 2 + second],
                    )
                )
    raws[0].start()
    for copy in slab_copies:
        copy.start()
    for copies in wait_strip.values():
        for copy in copies:
            copy.start()
    for copy in raws[1:]:
        copy.start()
    children = [
        pltpu.make_async_copy(front.at[2 * BLK :, BLK:], base, child_sem.at[0]),
        pltpu.make_async_copy(first, child.at[:, :, :, pl.ds(0, BLK)], child_sem.at[1]),
        pltpu.make_async_copy(rest, child.at[:, :, :, pl.ds(BLK, 3 * BLK)], child_sem.at[2]),
    ]
    for copy in children:
        copy.start()
    for copy in slab_copies:
        copy.wait()
    panel_out[: 2 * BLK, :] = jnp.zeros((2 * BLK, BLK), F32)
    for k in range(PW // STEP):
        known = STEP * k
        if k % 2 == 0:
            raws[k // 2].wait()
        for copy in wait_strip.get(known, ()):
            copy.wait()
        strip = max(n for n, (start, _) in enumerate(STRIPS) if start <= known)
        wh, wl = inverses[2 * strip], inverses[2 * strip + 1]
        inner = k - STRIPS[strip][0] // STEP
        here = slice(known, known + STEP)
        value = yraw[here, :]
        if k:
            value = value - pairs(dot_nn, high[here, :known], low[here, :known], yh[:known, :], yl[:known, :])
        vh, vl = split(value)
        got = pairs(dot_nn, wh[inner], wl[inner], vh, vl)
        yh[here, :], yl[here, :] = split(got)

        def tile(t, carry, k=k, known=known, here=here, wh=wh, wl=wl, inner=inner):
            rows = pl.ds(pl.multiple_of(t * 512, 512), 512)
            value = jnp.concatenate([raw[2 * k, rows, :], raw[2 * k + 1, rows, :]], axis=1)
            if k:
                value = value - pairs(dot_nt, xh[rows, :known], xl[rows, :known], high[here, :known], low[here, :known])
            vh, vl = split(value)
            got = pairs(dot_nt, vh, vl, wh[inner], wl[inner])
            xh[rows, here], xl[rows, here] = split(got)
            for side in range(2):

                @pl.when(col == 2 * k + side)
                def _():
                    panel_out[pl.ds(pl.multiple_of(2 * BLK + t * 512, BLK), 512), :] = got[:, side * BLK : (side + 1) * BLK]

            return carry

        lax.fori_loop(0, raw.shape[1] // 512, tile, 0)
    lanes = pl.ds(pl.multiple_of(col * BLK, BLK), BLK)
    for second in range(2):
        block_row = row + 8 * second

        @pl.when(block_row >= col)
        def _():
            rows = pl.ds(pl.multiple_of(block_row * BLK, BLK), BLK)
            panel_out[second * BLK : (second + 1) * BLK, :] = high[rows, lanes].astype(F32) + low[rows, lanes].astype(F32)

    trailing[: 2 * BLK, :] = jnp.zeros((2 * BLK, trailing.shape[1]), F32)
    trailing[:, :BLK] = jnp.zeros((trailing.shape[0], BLK), F32)

    for copy in children:
        copy.wait()

    def assemble(q, carry):
        rows = pl.ds(pl.multiple_of(q * BLK, BLK), BLK)
        out = pl.ds(pl.multiple_of((q + 2) * BLK, BLK), BLK)
        for n in range(1, 5):
            total = base[rows, (n - 1) * BLK : n * BLK]
            for k in range(2):
                at = source[k, q + 2]
                use = at >= 0
                at = jnp.maximum(at, 0)
                for sel, j in ((1, n), (2, n - 1)):
                    if j < 4:
                        block = child[at, q & 1, :, j * BLK : (j + 1) * BLK]
                        total = total + jnp.where(use & (colsel[k, n] == sel), block, F32(0))
            trailing[out, n * BLK : (n + 1) * BLK] = total
        return carry

    lax.fori_loop(0, 8, assemble, 0)

    def update(t, carry):
        rows = pl.ds(pl.multiple_of(t * 512, 512), 512)
        out = pl.ds(pl.multiple_of(2 * BLK + t * 512, STEP), 512)
        trailing[out, BLK:] = trailing[out, BLK:] - pairs(dot_nn, xh[rows, :], xl[rows, :], yh[...], yl[...])
        return carry

    lax.fori_loop(0, raw.shape[1] // 512, update, 0)


def solve(place, source, colsel, strips, inverses, slabs, panel_rows, front, first, rest):
    rows, cols = front.shape
    under = rows - 2 * BLK
    return pl.pallas_call(
        solve_kernel,
        out_shape=[jax.ShapeDtypeStruct((rows, BLK), F32), jax.ShapeDtypeStruct((rows, cols), F32)],
        in_specs=[SMEM] * 3 + [ANY] * len(strips) + [VMEM] * len(inverses) + [ANY] * 12,
        out_specs=[VMEM, VMEM],
        scratch_shapes=[
            pltpu.VMEM((PW, PW), BF16),
            pltpu.VMEM((PW, PW), BF16),
            pltpu.VMEM((under, PW), BF16),
            pltpu.VMEM((under, PW), BF16),
            pltpu.VMEM((PW, cols - BLK), BF16),
            pltpu.VMEM((PW, cols - BLK), BF16),
            pltpu.VMEM((16, under, BLK), F32),
            pltpu.VMEM((PW, cols - BLK), F32),
            pltpu.VMEM((under, cols - BLK), F32),
            pltpu.VMEM((8, 2, BLK, 4 * BLK), F32),
            pltpu.SemaphoreType.DMA((len(strips),)),
            pltpu.SemaphoreType.DMA((4,)),
            pltpu.SemaphoreType.DMA((16,)),
            pltpu.SemaphoreType.DMA((3,)),
        ],
        compiler_params=PARAMS,
        name="solve",
    )(place, source, colsel, *strips, *inverses, *slabs, panel_rows, front, first, rest)


def local(front, updates, maps):
    row_at = lax.axis_index("row")
    col_at = lax.axis_index("col")
    place = jnp.stack([row_at // 2, (col_at // 8) * 2 + row_at % 2, (col_at // 2) % 4, col_at % 2]).astype(jnp.int32)
    slots = maps >> 4
    row_slots = lax.dynamic_index_in_dim(slots.reshape(2, 2, 8, 4), row_at, 2, keepdims=False)
    col_slots = lax.dynamic_index_in_dim(slots.reshape(2, 16, 4), col_at, 1, keepdims=False)

    slot = jnp.arange(5)
    own = jnp.pad(row_slots, ((0, 0), (0, 0), (0, 1)), constant_values=-1) == slot
    prior = jnp.pad(row_slots, ((0, 0), (0, 0), (1, 0)), constant_values=-1) == slot
    source = jnp.where(own, slot, jnp.where(prior, slot - 1, -8)) + 4 * jnp.arange(2)[:, None, None]
    source = source.transpose(0, 2, 1).reshape(2, 10).astype(jnp.int32)
    own = jnp.pad(col_slots, ((0, 0), (0, 1)), constant_values=-1) == slot
    prior = jnp.pad(col_slots, ((0, 0), (1, 0)), constant_values=-1) == slot
    colsel = jnp.where(own, 1, jnp.where(prior, 2, 0)).astype(jnp.int32)

    def exchange(part):
        outgoing = part.reshape(2, 8, BLK, part.shape[1]).transpose(1, 0, 2, 3)
        return lax.all_to_all(outgoing, "row", split_axis=0, concat_axis=0, tiled=True)

    first = exchange(updates[:, :BLK])
    meets = col_slots[:, 0] == 0
    panel = front[:, :BLK].reshape(5, 2, BLK, BLK)
    parts = []
    for m in range(5):
        total = panel[m]
        for child in range(2):
            for a in (m, m - 1):
                if 0 <= a < 4:
                    hit = (row_slots[child, :, a] == m) & meets[child]
                    total = total + jnp.where(hit[:, None, None], first[4 * child + a], F32(0))
        parts.append(total)
    corner = parts[0].reshape(2 * BLK, BLK)
    under = jnp.stack(parts[1:]).reshape(8 * BLK, BLK)
    pieces, late = gather_leading(corner, place[1], place[3])

    tokens = [piece[0, 0, 0, 0, 0] for piece in pieces[5:]]
    panel_rows = lax.all_gather(settled(under, *tokens), "col", axis=0, tiled=True).reshape(16, 8 * BLK, BLK)
    late = around(settled(late, *tokens), 2)
    rest = exchange(settled(updates[:, BLK:], *tokens))

    strips, inverses = [], []

    def factor(call, place, pieces):
        got = factor_strip(call, place, pieces, strips)
        strips.extend(got[:2])
        inverses.extend(got[2:])
        return got[2][0, 0, 0].astype(F32)

    token = factor(0, place, pieces)
    late = settled(jnp.stack(late), token)
    late = [late, move(late, SWAP)]
    head = front[: 2 * BLK, BLK:].reshape(2, BLK, 4, BLK)
    for child in range(2):
        blocks = jnp.concatenate([first[4 * child], rest[4 * child]], axis=2).reshape(2, BLK, 4, BLK)
        ahead = jnp.concatenate([blocks[:, :, 1:], jnp.zeros((2, BLK, 1, BLK), F32)], axis=2)
        use = (row_slots[child, :, 0] == 0)[:, None, None, None]
        sel = colsel[child, 1:][None, None, :, None]
        head = head + jnp.where(use & (sel == 1), ahead, F32(0)) + jnp.where(use & (sel == 2), blocks, F32(0))
    head = settled(head.reshape(2 * BLK, 4 * BLK), token)
    slabs = []
    for dx in range(4):
        for dl in range(2):
            if dx == 0 and dl == 0:
                slabs.append(head)
                continue
            there = [(r, ((r // 2 - dx) % 4) * 2 + (r + dl) % 2) for r in range(8)]
            slabs.append(lax.ppermute(head, "row", there))
    factor(1, settled(place, head[0, 0]), late)
    factor(2, place, late)
    return tuple(solve(place, source, colsel, strips, inverses, slabs, panel_rows, front, first, rest))


def solution(mesh):
    in_specs = (P("row", "col"), P("row", "col"), P())
    out_specs = (P("row", "col"), P("row", "col"))
    return jax.shard_map(local, mesh=mesh, in_specs=in_specs, out_specs=out_specs, check_vma=False)
```

profile of v0, /device:TPU:10, one launch (start us, length us, event | category | flops | bytes accessed | tf_op | source)
XLA Modules:
  0.0 328.7 jit_solution(15624706420727389825)
XLA Ops:
  7.2 1.2 slice-done
  8.4 1.1 copy.17
  9.5 5.7 %all-to-all-start = ((f32[8,2,128,128]{3,2,1,0:T(8,128)}), f32[8,2,128,128]{3,2,1,0:T(8,128)S(1)}, u32[]{:S(2)}, u32[]{:S(2)}) async-start(f32[8,2,128,128]{3,2,1,0:T(8,128)} %bitcast.91), calls=%async_computation | async-start | bytes 2097152 | tf_op jit(solution)/shard_map/all_to_all | solution.py:532
  16.0 2.3 and_reduce_fusion.13
  18.3 1.3 broadcast_and_fusion.4
  19.6 1.9 fusion.7
  21.4 7.4 %all-to-all-done.refs_22_ = f32[8,2,128,128]{3,2,1,0:T(8,128)S(1)} async-done(((f32[8,2,128,128]{3,2,1,0:T(8,128)}), f32[8,2,128,128]{3,2,1,0:T(8,128)S(1)}, u32[]{:S(2)}, u32[]{:S(2)}) %all-to-all-start) | async-done | bytes 1048608 | tf_op jit(solution)/shard_map/all_to_all | solution.py:532
  29.1 1.2 collective-permute-done
  30.4 1.3 collective-permute-start.1
  31.6 2.3 collective-permute-start.2
  33.9 1.4 collective-permute-start.3
  36.3 4.0 %collective-permute-done.2 = f32[2,128,128]{2,1,0:T(8,128)S(1)} collective-permute-done((f32[2,128,128]{2,1,0:T(8,128)S(1)}, f32[2,128,128]{2,1,0:T(8,128)S(1)}, u32[]{:S(2)}, u32[]{:S(2)}) %collective-permute-start.2) | collective-permute-done | bytes 131104 | tf_op jit(solution)/shard_map/ppermute | solution.py:36
  41.1 2.0 collective-permute-start.4
  43.1 2.2 collective-permute-start.5
  45.3 1.8 collective-permute-start.6
  47.1 5.3 %collective-permute-done.4 = f32[4,2,128,128]{3,2,1,0:T(8,128)S(1)} collective-permute-done((f32[4,2,128,128]{3,2,1,0:T(8,128)S(1)}, f32[4,2,128,128]{3,2,1,0:T(8,128)S(1)}, u32[]{:S(2)}, u32[]{:S(2)}) %collective-permute-start.4) | collective-permute-done | bytes 524320 | tf_op jit(solution)/shard_map/ppermute | solution.py:36
  52.4 5.3 %collective-permute-done.5 = f32[4,2,128,128]{3,2,1,0:T(8,128)S(1)} collective-permute-done((f32[4,2,128,128]{3,2,1,0:T(8,128)S(1)}, f32[4,2,128,128]{3,2,1,0:T(8,128)S(1)}, u32[]{:S(2)}, u32[]{:S(2)}) %collective-permute-start.5) | collective-permute-done | bytes 524320 | tf_op jit(solution)/shard_map/ppermute | solution.py:36
  57.7 1.8 collective-permute-done.6
  61.1 1.7 collective-permute-start.8
  62.8 1.6 collective-permute-start.9
  64.4 11.5 %collective-permute-done.7.refs_1_ = f32[4,2,2,128,128]{4,3,2,1,0:T(8,128)} collective-permute-done((f32[4,2,2,128,128]{4,3,2,1,0:T(8,128)}, f32[4,2,2,128,128]{4,3,2,1,0:T(8,128)}, u32[]{:S(2)}, u32[]{:S(2)}) %collective-permute-start.7) | collective-permute-done | bytes 1048608 | tf_op jit(solution)/shard_map/ppermute | solution.py:36
  76.2 8.2 %collective-permute-start.12 = (f32[4,2,2,128,128]{4,3,2,1,0:T(8,128)}, f32[4,2,2,128,128]{4,3,2,1,0:T(8,128)}, u32[]{:S(2)}, u32[]{:S(2)}) collective-permute-start(f32[4,2,2,128,128]{4,3,2,1,0:T(8,128)} %collective-permute-done.8.refs_2_), channel_id=1, source_target_pairs={{0,1},{1,0},{2,3},{3,2},{4,5},{5,4},{6,7},{7,6},{16,17},{17,16},{1... | collective-permute-start | bytes 3145736 | tf_op jit(solution)/shard_map/ppermute | solution.py:36
  84.4 4.3 %collective-permute-done.9.refs_3_ = f32[4,2,2,128,128]{4,3,2,1,0:T(8,128)} collective-permute-done((f32[4,2,2,128,128]{4,3,2,1,0:T(8,128)}, f32[4,2,2,128,128]{4,3,2,1,0:T(8,128)}, u32[]{:S(2)}, u32[]{:S(2)}) %collective-permute-start.9) | collective-permute-done | bytes 1048608 | tf_op jit(solution)/shard_map/ppermute | solution.py:36
  90.9 1.4 select_add_fusion.3
  92.4 1.2 slice.228
  94.2 1.2 slice.229
  96.1 1.2 slice.230
  98.8 1.4 collective-permute-start.15
  100.2 1.8 collective-permute-start.16
  103.2 2.1 slice_select_fusion
  105.3 1.9 copy.16
  107.2 8.4 %all-to-all-start.1 = ((f32[8,2,128,384]{3,2,1,0:T(8,128)}), f32[8,2,128,384]{3,2,1,0:T(8,128)S(1)}, u32[]{:S(2)}, u32[]{:S(2)}) async-start(f32[8,2,128,384]{3,2,1,0:T(8,128)} %bitcast.93), calls=%async_computation.1 | async-start | bytes 6291456 | tf_op jit(solution)/shard_map/all_to_all | solution.py:532
  115.6 54.8 %factor0.1 = (bf16[2048,1024]{1,0:T(8,128)(2,1)}, bf16[2048,1024]{1,0:T(8,128)(2,1)}, bf16[4,256,256]{2,1,0:T(8,128)(2,1)}, bf16[4,256,256]{2,1,0:T(8,128)(2,1)}) custom-call(s32[4]{0:T(128)} %pad_add_fusion.place, f32[4,2,2,128,128]{4,3,2,1,0:T(8,128)} %slice.227.refs_0_, f32[4,2,2,128,128]{4,3,2,1,0:T(8,128)} %collective-permute-done.7.refs_1_, ...), custom_call_target="tpu_custom_call" | custom-call | flops 71680000000 | bytes 100000000 | tf_op jit(solution)/shard_map/factor0/pallas_call | solution.py:335
  170.4 1.1 slice.190
  172.1 3.1 maximum_select_fusion.refs_0_
  175.2 1.9 slice.191
  177.1 2.1 reshape.419
  180.8 1.9 pad_maximum_fusion.2
  182.8 2.0 reshape.421
  184.8 2.0 slice.232
  186.8 1.1 pad_maximum_fusion.3
  188.2 1.1 add_select_fusion
  190.5 4.1 %collective-permute-start.21 = (f32[256,512]{1,0:T(8,128)S(1)}, f32[256,512]{1,0:T(8,128)S(1)}, u32[]{:S(2)}, u32[]{:S(2)}) collective-permute-start(f32[256,512]{1,0:T(8,128)S(1)} %bitcast.109), channel_id=1, source_target_pairs={{0,112},{16,96},{32,16},{48,0},{64,48},{80,32},{96,80},{112,64},{1... | collective-permute-start | bytes 1572872 | tf_op jit(solution)/shard_map/ppermute | solution.py:581
  196.1 15.6 %collective-permute-start.23 = (f32[256,512]{1,0:T(8,128)S(1)}, f32[256,512]{1,0:T(8,128)S(1)}, u32[]{:S(2)}, u32[]{:S(2)}) collective-permute-start(f32[256,512]{1,0:T(8,128)S(1)} %bitcast.111), channel_id=1, source_target_pairs={{0,80},{16,64},{32,112},{48,96},{64,16},{80,0},{96,48},{112,32},{1... | collective-permute-start | bytes 1572872 | tf_op jit(solution)/shard_map/ppermute | solution.py:581
  211.7 29.1 %factor1.1 = (bf16[1024,512]{1,0:T(8,128)(2,1)}, bf16[1024,512]{1,0:T(8,128)(2,1)}, bf16[2,256,256]{2,1,0:T(8,128)(2,1)}, bf16[2,256,256]{2,1,0:T(8,128)(2,1)}) custom-call(s32[4]{0:T(128)} %broadcast_select_fusion.place, f32[4,4,2,128,128]{4,3,2,1,0:T(8,128)} %maximum_select_fusion.refs_0_, f32[4,4,2,128,128]{4,3,2,1,0:T(8,128)} %collective-permute-done.18.refs_1_, ...), custom_call_target="tpu_custom_call" | custom-call | flops 35840000000 | bytes 100000000 | tf_op jit(solution)/shard_map/factor1/pallas_call | solution.py:335
  240.9 1.7 collective-permute-start.25
  242.6 25.1 %factor2.1 = (bf16[512,512]{1,0:T(8,128)(2,1)}, bf16[512,512]{1,0:T(8,128)(2,1)}, bf16[2,256,256]{2,1,0:T(8,128)(2,1)}, bf16[2,256,256]{2,1,0:T(8,128)(2,1)}) custom-call(s32[4]{0:T(128)} %pad_add_fusion.place, f32[4,4,2,128,128]{4,3,2,1,0:T(8,128)} %maximum_select_fusion.refs_0_, f32[4,4,2,128,128]{4,3,2,1,0:T(8,128)} %collective-permute-done.18.refs_1_, ...), custom_call_target="tpu_custom_call" | custom-call | flops 35840000000 | bytes 100000000 | tf_op jit(solution)/shard_map/factor2/pallas_call | solution.py:335
  269.1 52.5 %solve.1 = (f32[1280,128]{1,0:T(8,128)}, f32[1280,640]{1,0:T(8,128)}) custom-call(s32[4]{0:T(128)} %pad_add_fusion.place, s32[2,10]{1,0:T(2,128)} %reshape.416.source, s32[2,5]{1,0:T(2,128)} %copy-done.13, bf16[2048,1024]{1,0:T(8,128)(2,1)} %get-tuple-element.14.refs_2_.refs_0_, bf16[2048,1024]{1,0:T(8,128)(2,1)} %get-tuple-element.15.refs_3_.refs_1_, ...), custom_call_target="tpu_custom_call" | custom-call | tf_op jit(solution)/shard_map/solve/pallas_call | solution.py:487
  (105 shorter events, 14.3 us)
Async XLA Ops:
  7.2 1.2 slice-start
  8.4 6.8 %copy-start.16 = (s32[2,64]{1,0:T(2,128)S(1)}, s32[2,64]{1,0:T(2,128)}, u32[]{:S(2)}) copy-start(s32[2,64]{1,0:T(2,128)} %param.5) | copy-start | bytes 1540
  9.5 19.4 %all-to-all-start = ((f32[8,2,128,128]{3,2,1,0:T(8,128)}), f32[8,2,128,128]{3,2,1,0:T(8,128)S(1)}, u32[]{:S(2)}, u32[]{:S(2)}) async-start(f32[8,2,128,128]{3,2,1,0:T(8,128)} %bitcast.91), calls=%async_computation | async-start | bytes 2097152 | tf_op jit(solution)/shard_map/all_to_all | solution.py:532
  15.2 253.5 %all-gather.2.cloned.1.call-start = ((), (), s32[]{:S(2)}) async-start(), calls=%async_computation.2 | async-start | bytes 8912896 | tf_op jit(solution)/shard_map/all_gather | solution.py:551
  28.9 62.0 %copy-start.1 = (f32[8,2,128,128]{3,2,1,0:T(8,128)}, f32[8,2,128,128]{3,2,1,0:T(8,128)S(1)}, u32[]{:S(2)}) copy-start(f32[8,2,128,128]{3,2,1,0:T(8,128)S(1)} %all-to-all-done.refs_22_) | copy-start | bytes 3145732
  29.0 1.3 collective-permute-start
  30.4 5.9 %collective-permute-start.1 = (f32[2,128,128]{2,1,0:T(8,128)S(1)}, f32[2,128,128]{2,1,0:T(8,128)S(1)}, u32[]{:S(2)}, u32[]{:S(2)}) collective-permute-start(f32[2,128,128]{2,1,0:T(8,128)S(1)} %pad_maximum_fusion.4), channel_id=1, source_target_pairs={{0,24},{1,25},{2,26},{3,27},{4,28},{5,29},{6,30},{7,31},{16,0},{17... | collective-permute-start | bytes 393224 | tf_op jit(solution)/shard_map/ppermute | solution.py:36
  31.6 8.6 %collective-permute-start.2 = (f32[2,128,128]{2,1,0:T(8,128)S(1)}, f32[2,128,128]{2,1,0:T(8,128)S(1)}, u32[]{:S(2)}, u32[]{:S(2)}) collective-permute-start(f32[2,128,128]{2,1,0:T(8,128)S(1)} %pad_maximum_fusion.4), channel_id=1, source_target_pairs={{0,8},{1,9},{2,10},{3,11},{4,12},{5,13},{6,14},{7,15},{16,24},{17,... | collective-permute-start | bytes 393224 | tf_op jit(solution)/shard_map/ppermute | solution.py:36
  33.9 7.0 %collective-permute-start.3 = (f32[2,128,128]{2,1,0:T(8,128)S(1)}, f32[2,128,128]{2,1,0:T(8,128)S(1)}, u32[]{:S(2)}, u32[]{:S(2)}) collective-permute-start(f32[2,128,128]{2,1,0:T(8,128)S(1)} %pad_maximum_fusion.4), channel_id=1, source_target_pairs={{0,16},{1,17},{2,18},{3,19},{4,20},{5,21},{6,22},{7,23},{16,8},{17... | collective-permute-start | bytes 393224 | tf_op jit(solution)/shard_map/ppermute | solution.py:36
  41.1 11.3 %collective-permute-start.4 = (f32[4,2,128,128]{3,2,1,0:T(8,128)S(1)}, f32[4,2,128,128]{3,2,1,0:T(8,128)S(1)}, u32[]{:S(2)}, u32[]{:S(2)}) collective-permute-start(f32[4,2,128,128]{3,2,1,0:T(8,128)S(1)} %get-tuple-element.56), channel_id=1, source_target_pairs={{0,2},{1,33},{2,4},{3,35},{4,6},{5,37},{6,0},{7,39},{16,18},{17,49... | collective-permute-start | bytes 1572872 | tf_op jit(solution)/shard_map/ppermute | solution.py:36
  43.1 14.6 %collective-permute-start.5 = (f32[4,2,128,128]{3,2,1,0:T(8,128)S(1)}, f32[4,2,128,128]{3,2,1,0:T(8,128)S(1)}, u32[]{:S(2)}, u32[]{:S(2)}) collective-permute-start(f32[4,2,128,128]{3,2,1,0:T(8,128)S(1)} %get-tuple-element.56), channel_id=1, source_target_pairs={{0,6},{1,97},{2,0},{3,99},{4,2},{5,101},{6,4},{7,103},{16,22},{17,... | collective-permute-start | bytes 1572872 | tf_op jit(solution)/shard_map/ppermute | solution.py:36
  45.3 14.2 %collective-permute-start.6 = (f32[4,2,128,128]{3,2,1,0:T(8,128)S(1)}, f32[4,2,128,128]{3,2,1,0:T(8,128)S(1)}, u32[]{:S(2)}, u32[]{:S(2)}) collective-permute-start(f32[4,2,128,128]{3,2,1,0:T(8,128)S(1)} %get-tuple-element.56), channel_id=1, source_target_pairs={{0,4},{1,65},{2,6},{3,67},{4,0},{5,69},{6,2},{7,71},{16,20},{17,81... | collective-permute-start | bytes 1572872 | tf_op jit(solution)/shard_map/ppermute | solution.py:36
  60.7 15.1 %collective-permute-start.7 = (f32[4,2,2,128,128]{4,3,2,1,0:T(8,128)}, f32[4,2,2,128,128]{4,3,2,1,0:T(8,128)}, u32[]{:S(2)}, u32[]{:S(2)}) collective-permute-start(f32[4,2,2,128,128]{4,3,2,1,0:T(8,128)} %slice.227.refs_0_), channel_id=1, source_target_pairs={{0,32},{1,3},{2,34},{3,5},{4,36},{5,7},{6,38},{7,1},{16,48},{17,19... | collective-permute-start | bytes 3145736 | tf_op jit(solution)/shard_map/ppermute | solution.py:36
  61.1 15.1 %collective-permute-start.8 = (f32[4,2,2,128,128]{4,3,2,1,0:T(8,128)}, f32[4,2,2,128,128]{4,3,2,1,0:T(8,128)}, u32[]{:S(2)}, u32[]{:S(2)}) collective-permute-start(f32[4,2,2,128,128]{4,3,2,1,0:T(8,128)} %slice.227.refs_0_), channel_id=1, source_target_pairs={{0,96},{1,7},{2,98},{3,1},{4,100},{5,3},{6,102},{7,5},{16,112},{17... | collective-permute-start | bytes 3145736 | tf_op jit(solution)/shard_map/ppermute | solution.py:36
  62.8 25.9 %collective-permute-start.9 = (f32[4,2,2,128,128]{4,3,2,1,0:T(8,128)}, f32[4,2,2,128,128]{4,3,2,1,0:T(8,128)}, u32[]{:S(2)}, u32[]{:S(2)}) collective-permute-start(f32[4,2,2,128,128]{4,3,2,1,0:T(8,128)} %slice.227.refs_0_), channel_id=1, source_target_pairs={{0,64},{1,5},{2,66},{3,7},{4,68},{5,1},{6,70},{7,3},{16,80},{17,21... | collective-permute-start | bytes 3145736 | tf_op jit(solution)/shard_map/ppermute | solution.py:36
  75.9 16.5 %collective-permute-start.11 = (f32[4,2,2,128,128]{4,3,2,1,0:T(8,128)}, f32[4,2,2,128,128]{4,3,2,1,0:T(8,128)}, u32[]{:S(2)}, u32[]{:S(2)}) collective-permute-start(f32[4,2,2,128,128]{4,3,2,1,0:T(8,128)} %collective-permute-done.7.refs_1_), channel_id=1, source_target_pairs={{0,1},{1,0},{2,3},{3,2},{4,5},{5,4},{6,7},{7,6},{16,17},{17,16},{1... | collective-permute-start | bytes 3145736 | tf_op jit(solution)/shard_map/ppermute | solution.py:36
  76.2 18.1 %collective-permute-start.12 = (f32[4,2,2,128,128]{4,3,2,1,0:T(8,128)}, f32[4,2,2,128,128]{4,3,2,1,0:T(8,128)}, u32[]{:S(2)}, u32[]{:S(2)}) collective-permute-start(f32[4,2,2,128,128]{4,3,2,1,0:T(8,128)} %collective-permute-done.8.refs_2_), channel_id=1, source_target_pairs={{0,1},{1,0},{2,3},{3,2},{4,5},{5,4},{6,7},{7,6},{16,17},{17,16},{1... | collective-permute-start | bytes 3145736 | tf_op jit(solution)/shard_map/ppermute | solution.py:36
  88.7 7.4 %collective-permute-start.13 = (f32[4,2,2,128,128]{4,3,2,1,0:T(8,128)}, f32[4,2,2,128,128]{4,3,2,1,0:T(8,128)}, u32[]{:S(2)}, u32[]{:S(2)}) collective-permute-start(f32[4,2,2,128,128]{4,3,2,1,0:T(8,128)} %collective-permute-done.9.refs_3_), channel_id=1, source_target_pairs={{0,1},{1,0},{2,3},{3,2},{4,5},{5,4},{6,7},{7,6},{16,17},{17,16},{1... | collective-permute-start | bytes 3145736 | tf_op jit(solution)/shard_map/ppermute | solution.py:36
  88.7 2.2 copy-start.12
  88.8 9.2 %collective-permute-start.14 = (f32[4,2,128,128]{3,2,1,0:T(8,128)S(1)}, f32[4,2,128,128]{3,2,1,0:T(8,128)S(1)}, u32[]{:S(2)}, u32[]{:S(2)}) collective-permute-start(f32[4,2,128,128]{3,2,1,0:T(8,128)S(1)} %maximum_bitcast_fusion.1), channel_id=1, source_target_pairs={{0,1},{1,0},{2,3},{3,2},{4,5},{5,4},{6,7},{7,6},{16,17},{17,16},{1... | collective-permute-start | bytes 1572872 | tf_op jit(solution)/shard_map/ppermute | solution.py:36
  90.8 24.8 %collective-permute-start.10 = (f32[4,2,2,128,128]{4,3,2,1,0:T(8,128)}, f32[4,2,2,128,128]{4,3,2,1,0:T(8,128)}, u32[]{:S(2)}, u32[]{:S(2)}) collective-permute-start(f32[4,2,2,128,128]{4,3,2,1,0:T(8,128)} %slice.227.refs_0_), channel_id=1, source_target_pairs={{0,1},{1,0},{2,3},{3,2},{4,5},{5,4},{6,7},{7,6},{16,17},{17,16},{1... | collective-permute-start | bytes 3145736 | tf_op jit(solution)/shard_map/ppermute | solution.py:36
  98.8 73.3 %collective-permute-start.15 = (f32[4,2,128,128]{3,2,1,0:T(8,128)}, f32[4,2,128,128]{3,2,1,0:T(8,128)}, u32[]{:S(2)}, u32[]{:S(2)}) collective-permute-start(f32[4,2,128,128]{3,2,1,0:T(8,128)} %fusion.1), channel_id=1, source_target_pairs={{0,2},{1,3},{2,4},{3,5},{4,6},{5,7},{6,0},{7,1},{16,18},{17,19},{1... | collective-permute-start | bytes 1572872 | tf_op jit(solution)/shard_map/ppermute | solution.py:36
  100.2 71.9 %collective-permute-start.16 = (f32[4,2,128,128]{3,2,1,0:T(8,128)}, f32[4,2,128,128]{3,2,1,0:T(8,128)}, u32[]{:S(2)}, u32[]{:S(2)}) collective-permute-start(f32[4,2,128,128]{3,2,1,0:T(8,128)} %fusion.1), channel_id=1, source_target_pairs={{0,6},{1,7},{2,0},{3,1},{4,2},{5,3},{6,4},{7,5},{16,22},{17,23},{1... | collective-permute-start | bytes 1572872 | tf_op jit(solution)/shard_map/ppermute | solution.py:36
  102.1 70.1 %collective-permute-start.17 = (f32[4,2,128,128]{3,2,1,0:T(8,128)}, f32[4,2,128,128]{3,2,1,0:T(8,128)}, u32[]{:S(2)}, u32[]{:S(2)}) collective-permute-start(f32[4,2,128,128]{3,2,1,0:T(8,128)} %fusion.1), channel_id=1, source_target_pairs={{0,4},{1,5},{2,6},{3,7},{4,0},{5,1},{6,2},{7,3},{16,20},{17,21},{1... | collective-permute-start | bytes 1572872 | tf_op jit(solution)/shard_map/ppermute | solution.py:36
  107.2 73.6 %all-to-all-start.1 = ((f32[8,2,128,384]{3,2,1,0:T(8,128)}), f32[8,2,128,384]{3,2,1,0:T(8,128)S(1)}, u32[]{:S(2)}, u32[]{:S(2)}) async-start(f32[8,2,128,384]{3,2,1,0:T(8,128)} %bitcast.93), calls=%async_computation.1 | async-start | bytes 6291456 | tf_op jit(solution)/shard_map/all_to_all | solution.py:532
  175.2 20.9 %collective-permute-start.18 = (f32[4,4,2,128,128]{4,3,2,1,0:T(8,128)}, f32[4,4,2,128,128]{4,3,2,1,0:T(8,128)}, u32[]{:S(2)}, u32[]{:S(2)}) collective-permute-start(f32[4,4,2,128,128]{4,3,2,1,0:T(8,128)} %maximum_select_fusion.refs_0_), channel_id=1, source_target_pairs={{0,1},{1,0},{2,3},{3,2},{4,5},{5,4},{6,7},{7,6},{16,17},{17,16},{1... | collective-permute-start | bytes 6291464 | tf_op jit(solution)/shard_map/ppermute | solution.py:36
  180.0 6.7 %copy-start.13 = (s32[2,5]{1,0:T(2,128)}, s32[2,5]{1,0:T(2,128)S(1)}, u32[]{:S(2)}) copy-start(s32[2,5]{1,0:T(2,128)S(1)} %compare_select_fusion.3.colsel) | copy-start | bytes 124
  180.8 6.0 %copy-start = (f32[8,2,128,384]{3,2,1,0:T(8,128)}, f32[8,2,128,384]{3,2,1,0:T(8,128)S(1)}, u32[]{:S(2)}) copy-start(f32[8,2,128,384]{3,2,1,0:T(8,128)S(1)} %all-to-all-done.1.refs_23_) | copy-start | bytes 9437188
  184.8 3.4 %copy-start.14 = (pred[2,4]{1,0:T(4,128)(4,1)S(1)}, pred[2,4]{1,0:T(4,128)(4,1)}, u32[]{:S(2)}) copy-start(pred[2,4]{1,0:T(4,128)(4,1)} %get-tuple-element.69) | copy-start | bytes 28
  184.8 3.4 %copy-start.15 = (pred[2,4]{1,0:T(4,128)(4,1)S(1)}, pred[2,4]{1,0:T(4,128)(4,1)}, u32[]{:S(2)}) copy-start(pred[2,4]{1,0:T(4,128)(4,1)} %get-tuple-element.72) | copy-start | bytes 28
  186.7 1.5 copy-start.2
  186.7 1.5 copy-start.4
  186.7 1.5 copy-start.5
  189.3 51.5 %copy-start.3 = (f32[32,8,4,128]{3,1,2,0:T(8,128)}, f32[32,8,4,128]{3,1,2,0:T(8,128)S(1)}, u32[]{:S(2)}) copy-start(f32[32,8,4,128]{3,1,2,0:T(8,128)S(1)} %copy.18) | copy-start | bytes 1572868
  189.9 50.9 %collective-permute-start.19 = (f32[256,512]{1,0:T(8,128)S(1)}, f32[256,512]{1,0:T(8,128)S(1)}, u32[]{:S(2)}, u32[]{:S(2)}) collective-permute-start(f32[256,512]{1,0:T(8,128)S(1)} %bitcast.107), channel_id=1, source_target_pairs={{0,16},{16,0},{32,48},{48,32},{64,80},{80,64},{96,112},{112,96},{1... | collective-permute-start | bytes 1572872 | tf_op jit(solution)/shard_map/ppermute | solution.py:581
  190.5 50.4 %collective-permute-start.20 = (f32[256,512]{1,0:T(8,128)S(1)}, f32[256,512]{1,0:T(8,128)S(1)}, u32[]{:S(2)}, u32[]{:S(2)}) collective-permute-start(f32[256,512]{1,0:T(8,128)S(1)} %bitcast.108), channel_id=1, source_target_pairs={{0,96},{16,112},{32,0},{48,16},{64,32},{80,48},{96,64},{112,80},{1... | collective-permute-start | bytes 1572872 | tf_op jit(solution)/shard_map/ppermute | solution.py:581
  190.5 77.2 %collective-permute-start.21 = (f32[256,512]{1,0:T(8,128)S(1)}, f32[256,512]{1,0:T(8,128)S(1)}, u32[]{:S(2)}, u32[]{:S(2)}) collective-permute-start(f32[256,512]{1,0:T(8,128)S(1)} %bitcast.109), channel_id=1, source_target_pairs={{0,112},{16,96},{32,16},{48,0},{64,48},{80,32},{96,80},{112,64},{1... | collective-permute-start | bytes 1572872 | tf_op jit(solution)/shard_map/ppermute | solution.py:581
  194.6 73.2 %collective-permute-start.22 = (f32[256,512]{1,0:T(8,128)S(1)}, f32[256,512]{1,0:T(8,128)S(1)}, u32[]{:S(2)}, u32[]{:S(2)}) collective-permute-start(f32[256,512]{1,0:T(8,128)S(1)} %bitcast.110), channel_id=1, source_target_pairs={{0,64},{16,80},{32,96},{48,112},{64,0},{80,16},{96,32},{112,48},{1... | collective-permute-start | bytes 1572872 | tf_op jit(solution)/shard_map/ppermute | solution.py:581
  196.1 71.7 %collective-permute-start.23 = (f32[256,512]{1,0:T(8,128)S(1)}, f32[256,512]{1,0:T(8,128)S(1)}, u32[]{:S(2)}, u32[]{:S(2)}) collective-permute-start(f32[256,512]{1,0:T(8,128)S(1)} %bitcast.111), channel_id=1, source_target_pairs={{0,80},{16,64},{32,112},{48,96},{64,16},{80,0},{96,48},{112,32},{1... | collective-permute-start | bytes 1572872 | tf_op jit(solution)/shard_map/ppermute | solution.py:581
  240.8 27.0 %copy-start.6 = (f32[256,512]{1,0:T(8,128)}, f32[256,512]{1,0:T(8,128)S(1)}, u32[]{:S(2)}) copy-start(f32[256,512]{1,0:T(8,128)S(1)} %collective-permute-done.19.refs_13_) | copy-start | bytes 1572868
  240.8 27.0 %collective-permute-start.24 = (f32[256,512]{1,0:T(8,128)S(1)}, f32[256,512]{1,0:T(8,128)S(1)}, u32[]{:S(2)}, u32[]{:S(2)}) collective-permute-start(f32[256,512]{1,0:T(8,128)S(1)} %bitcast.112), channel_id=1, source_target_pairs={{0,32},{16,48},{32,64},{48,80},{64,96},{80,112},{96,0},{112,16},{1... | collective-permute-start | bytes 1572872 | tf_op jit(solution)/shard_map/ppermute | solution.py:581
  240.9 26.9 %copy-start.7 = (f32[256,512]{1,0:T(8,128)}, f32[256,512]{1,0:T(8,128)S(1)}, u32[]{:S(2)}) copy-start(f32[256,512]{1,0:T(8,128)S(1)} %collective-permute-done.20.refs_14_) | copy-start | bytes 1572868
  240.9 27.8 %collective-permute-start.25 = (f32[256,512]{1,0:T(8,128)S(1)}, f32[256,512]{1,0:T(8,128)}, u32[]{:S(2)}, u32[]{:S(2)}) collective-permute-start(f32[256,512]{1,0:T(8,128)S(1)} %bitcast.113), channel_id=1, source_target_pairs={{0,48},{16,32},{32,80},{48,64},{64,112},{80,96},{96,16},{112,0},{1... | collective-permute-start | bytes 1572872 | tf_op jit(solution)/shard_map/ppermute | solution.py:581
  267.8 1.0 copy-start.8
  267.8 1.2 copy-start.9
  267.8 1.3 copy-start.10
  267.8 0.9 copy-start.11
Sparse Core Ops, SparseCore 0:
  103.3 106.6 all-gather.1
where the time goes:
time: 332 us; the launch traced here: 329 us
  Pallas kernels  162 us (49%)
  starting transfers between devices  63.5 us (19%)
  waiting for transfers between devices  42.8 us (13%)
  local copies, waits for them, and re-layouts  23.5 us (7%)
  other arithmetic  19.4 us (6%)
  between operations  18 us (5%)
    pallas_call x3, Pallas kernels, factor_strip(): pl.pallas_call(functools.partial(factor_kernel, call), out_shape=[strip,...  109 us
    pallas_call x1, Pallas kernels, solve(): pl.pallas_call(solve_kernel, out_shape=[jax.ShapeDtypeStruct((rows, BLK),...  52.5 us
    ppermute x19, waiting for transfers between devices, move(): return lax.ppermute(value, BOTH, pairs)  35.3 us
    ppermute x19, starting transfers between devices, move(): return lax.ppermute(value, BOTH, pairs)  27.1 us
    ppermute x7, starting transfers between devices, local(): slabs.append(lax.ppermute(head, 'row', there))  22.3 us
    all_to_all x2, starting transfers between devices, exchange(): lax.all_to_all(outgoing, 'row', split_axis=0, concat_axis=0, tiled=True)  14.1 us
    select_n x6, other arithmetic, settled(): return jnp.where(ready, value, jnp.zeros((), value.dtype))  8.54 us
    all_to_all x2, waiting for transfers between devices, exchange(): lax.all_to_all(outgoing, 'row', split_axis=0, concat_axis=0, tiled=True)  7.45 us
  transfers between devices with their start and end apart: 29, of which 11 were waited for; matrix products, arithmetic and copies ran while one was open for 11% of the time, Pallas kernels for 33%

commit v1 on v0

--- a/solution.py
+++ b/solution.py
@@ -46,9 +46,11 @@
     return out
 
 
-def settled(value, *tokens):
+def held(array, tokens):
+    array = lax.optimization_barrier(array)
     ready = functools.reduce(jnp.logical_and, [token <= F32(jnp.finfo(jnp.float32).max) for token in tokens])
-    return jnp.where(ready, value, jnp.zeros((), value.dtype))
+    at = (0,) * array.ndim
+    return array.at[at].set(jnp.where(ready, array[at], F32(0)))
 
 
 def gather_leading(corner, y_at, core_at):
@@ -250,26 +252,35 @@
         high[rows, cols] = h
         low[rows, cols] = l
 
+    def under(at, tile):
+        wide = (PW - start - at) // 512
+
+        def one(t, carry):
+            tile(pl.multiple_of(at + t * 512, STEP), 512)
+            return carry
+
+        lax.fori_loop(0, wide, one, 0)
+        if at + wide * 512 < PW - start:
+            tile(at + wide * 512, STEP)
+
     def before(kk):
         if kk and kk % 2 == 0:
             wait_lead(kk // 2)
         known = start + STEP * kk
         r0 = STEP * kk
-        tiles = (PW - start - r0) // STEP
-
-        def tile(t, carry):
-            at = pl.multiple_of(r0 + t * STEP, STEP)
-            rows = pl.ds(at, STEP)
-            whole = pl.ds(pl.multiple_of(start + at, STEP), STEP)
+
+        def tile(at, size):
+            rows = pl.ds(at, size)
+            whole = pl.ds(pl.multiple_of(start + at, STEP), size)
             value = jnp.concatenate([lead[2 * kk, whole, :], lead[2 * kk + 1, whole, :]], axis=1)
             if known > 0:
                 value = value - pairs(
                     dot_nt, high[rows, :known], low[rows, :known], high[r0 : r0 + STEP, :known], low[r0 : r0 + STEP, :known]
                 )
             c[rows, :] = value
-            return carry
-
-        lax.fori_loop(0, tiles, tile, 0)
+
+        tile(r0, STEP)
+        under(r0 + STEP, tile)
         diag[...] = c[r0 : r0 + BLK, :BLK]
 
     def between(kk):
@@ -295,15 +306,13 @@
         wh, wl = split(w)
         inv_high[kk] = wh
         inv_low[kk] = wl
-        tiles = (PW - start - r0) // STEP
-
-        def tile(t, carry):
-            rows = pl.ds(pl.multiple_of(r0 + t * STEP, STEP), STEP)
+
+        def tile(at, size):
+            rows = pl.ds(at, size)
             ch, cl = split(c[rows, :])
             put(rows, pl.ds(col, STEP), pairs(dot_nt, ch, cl, inv_high[kk], inv_low[kk]))
-            return carry
-
-        lax.fori_loop(1, tiles, tile, 0)
+
+        under(r0 + STEP, tile)
         for copy in outs(kk):
             copy.start()
 
@@ -357,6 +366,60 @@
     )(place, *pieces, *earlier)
 
 
+def head_kernel(hit, colsel, token, front, f0, f1, g0, g1, own, below, above, opposite, head, late, sems):
+    del token
+    copies = [pltpu.make_async_copy(ref, late.at[n], sems.at[n]) for n, ref in enumerate((own, below, above, opposite))]
+    for copy in copies:
+        copy.start()
+    for w in range(2):
+        rows = slice(w * BLK, (w + 1) * BLK)
+        for n in range(1, 5):
+            total = front[rows, n * BLK : (n + 1) * BLK]
+            for k, (first, rest) in enumerate(((f0, g0), (f1, g1))):
+                for sel, j in ((1, n), (2, n - 1)):
+                    if j < 4:
+                        block = first[0, w] if j == 0 else rest[0, w, :, (j - 1) * BLK : j * BLK]
+                        use = (hit[k, w] == 1) & (colsel[k, n] == sel)
+                        total = total + jnp.where(use, block, F32(0))
+            head[rows, (n - 1) * BLK : n * BLK] = total
+    for copy in copies:
+        copy.wait()
+
+
+def head_rows(hit, colsel, token, front, first, rest, late):
+    cols = front.shape[1]
+
+    def child(k):
+        return lambda i: (4 * k, 0, 0, 0)
+
+    return pl.pallas_call(
+        head_kernel,
+        grid=(1,),
+        out_shape=[
+            jax.ShapeDtypeStruct((2 * BLK, cols - BLK), F32),
+            jax.ShapeDtypeStruct((4, *late[0].shape), F32),
+        ],
+        in_specs=[
+            SMEM,
+            SMEM,
+            ANY,
+            pl.BlockSpec((2 * BLK, cols), lambda i: (0, 0)),
+            pl.BlockSpec((1, 2, BLK, BLK), child(0)),
+            pl.BlockSpec((1, 2, BLK, BLK), child(1)),
+            pl.BlockSpec((1, 2, BLK, 3 * BLK), child(0)),
+            pl.BlockSpec((1, 2, BLK, 3 * BLK), child(1)),
+            ANY,
+            ANY,
+            ANY,
+            ANY,
+        ],
+        out_specs=[pl.BlockSpec((2 * BLK, cols - BLK), lambda i: (0, 0)), ANY],
+        scratch_shapes=[pltpu.SemaphoreType.DMA((4,))],
+        compiler_params=PARAMS,
+        name="head",
+    )(hit, colsel, token, front, first, first, rest, rest, *late)
+
+
 def solve_kernel(place, source, colsel, *refs):
     n_strips = 2 * len(STRIPS)
     strips, inverses, refs = refs[:n_strips], refs[n_strips : 2 * n_strips], refs[2 * n_strips :]
@@ -366,13 +429,25 @@
     x, y, z, core = place[0], place[1], place[2], place[3]
     row = x * 2 + y % 2
     col = (y // 2) * 8 + z * 2 + core
-    wait_strip = {}
-    for n, (start, width) in enumerate(STRIPS):
-        rows, cols = pl.ds(start, PW - start), pl.ds(start, width)
-        wait_strip[start] = [
-            pltpu.make_async_copy(strips[2 * n + which], dest.at[rows, cols], sems.at[2 * n + which])
-            for which, dest in ((0, high), (1, low))
-        ]
+    blocks = PW // STEP
+    factor_rows = [[] for _ in range(blocks)]
+    for k in range(blocks):
+        for n, (start, width) in enumerate(STRIPS):
+            if start <= STEP * k:
+                cols = min(width, STEP * (k + 1) - start)
+                for which, dest in ((0, high), (1, low)):
+                    factor_rows[k].append(
+                        pltpu.make_async_copy(
+                            strips[2 * n + which].at[pl.ds(STEP * k - start, STEP), pl.ds(0, cols)],
+                            dest.at[pl.ds(STEP * k, STEP), pl.ds(start, cols)],
+                            sems.at[k, 2 * n + which],
+                        )
+                    )
+
+    def start_all(copies):
+        for copy in copies:
+            copy.start()
+
     raws = [pltpu.make_async_copy(panel_rows.at[pl.ds(4 * n, 4)], raw.at[pl.ds(4 * n, 4)], raw_sem.at[n]) for n in range(4)]
     slab_copies = []
     for dx in range(4):
@@ -387,21 +462,15 @@
                         slab_sem.at[(dx * 2 + dl) * 2 + second],
                     )
                 )
-    raws[0].start()
-    for copy in slab_copies:
-        copy.start()
-    for copies in wait_strip.values():
-        for copy in copies:
-            copy.start()
-    for copy in raws[1:]:
-        copy.start()
     children = [
         pltpu.make_async_copy(front.at[2 * BLK :, BLK:], base, child_sem.at[0]),
         pltpu.make_async_copy(first, child.at[:, :, :, pl.ds(0, BLK)], child_sem.at[1]),
         pltpu.make_async_copy(rest, child.at[:, :, :, pl.ds(BLK, 3 * BLK)], child_sem.at[2]),
     ]
-    for copy in children:
-        copy.start()
+    start_all(slab_copies)
+    raws[0].start()
+    for k in range(3):
+        start_all(factor_rows[k])
     for copy in slab_copies:
         copy.wait()
     panel_out[: 2 * BLK, :] = jnp.zeros((2 * BLK, BLK), F32)
@@ -409,7 +478,13 @@
         known = STEP * k
         if k % 2 == 0:
             raws[k // 2].wait()
-        for copy in wait_strip.get(known, ()):
+            if k // 2 + 1 < len(raws):
+                raws[k // 2 + 1].start()
+        if k + 3 < blocks:
+            start_all(factor_rows[k + 3])
+        if k == 5:
+            start_all(children)
+        for copy in factor_rows[k]:
             copy.wait()
         strip = max(n for n, (start, _) in enumerate(STRIPS) if start <= known)
         wh, wl = inverses[2 * strip], inverses[2 * strip + 1]
@@ -500,7 +575,7 @@
             pltpu.VMEM((PW, cols - BLK), F32),
             pltpu.VMEM((under, cols - BLK), F32),
             pltpu.VMEM((8, 2, BLK, 4 * BLK), F32),
-            pltpu.SemaphoreType.DMA((len(strips),)),
+            pltpu.SemaphoreType.DMA((PW // STEP, len(strips))),
             pltpu.SemaphoreType.DMA((4,)),
             pltpu.SemaphoreType.DMA((16,)),
             pltpu.SemaphoreType.DMA((3,)),
@@ -527,11 +602,13 @@
     prior = jnp.pad(col_slots, ((0, 0), (1, 0)), constant_values=-1) == slot
     colsel = jnp.where(own, 1, jnp.where(prior, 2, 0)).astype(jnp.int32)
 
-    def exchange(part):
-        outgoing = part.reshape(2, 8, BLK, part.shape[1]).transpose(1, 0, 2, 3)
+    def outgoing(part):
+        return part.reshape(2, 8, BLK, part.shape[1]).transpose(1, 0, 2, 3)
+
+    def exchange(outgoing):
         return lax.all_to_all(outgoing, "row", split_axis=0, concat_axis=0, tiled=True)
 
-    first = exchange(updates[:, :BLK])
+    first = exchange(outgoing(updates[:, :BLK]))
     meets = col_slots[:, 0] == 0
     panel = front[:, :BLK].reshape(5, 2, BLK, BLK)
     parts = []
@@ -548,9 +625,9 @@
     pieces, late = gather_leading(corner, place[1], place[3])
 
     tokens = [piece[0, 0, 0, 0, 0] for piece in pieces[5:]]
-    panel_rows = lax.all_gather(settled(under, *tokens), "col", axis=0, tiled=True).reshape(16, 8 * BLK, BLK)
-    late = around(settled(late, *tokens), 2)
-    rest = exchange(settled(updates[:, BLK:], *tokens))
+    panel_rows = lax.all_gather(held(under, tokens), "col", axis=0, tiled=True).reshape(16, 8 * BLK, BLK)
+    late = around(held(late, tokens), 2)
+    rest = exchange(held(outgoing(updates[:, BLK:]), tokens))
 
     strips, inverses = [], []
 
@@ -558,19 +635,11 @@
         got = factor_strip(call, place, pieces, strips)
         strips.extend(got[:2])
         inverses.extend(got[2:])
-        return got[2][0, 0, 0].astype(F32)
-
-    token = factor(0, place, pieces)
-    late = settled(jnp.stack(late), token)
+
+    factor(0, place, pieces)
+    hit = (row_slots[:, :, 0] == 0).astype(jnp.int32)
+    head, late = head_rows(hit, colsel, inverses[0], front, first, rest, late)
     late = [late, move(late, SWAP)]
-    head = front[: 2 * BLK, BLK:].reshape(2, BLK, 4, BLK)
-    for child in range(2):
-        blocks = jnp.concatenate([first[4 * child], rest[4 * child]], axis=2).reshape(2, BLK, 4, BLK)
-        ahead = jnp.concatenate([blocks[:, :, 1:], jnp.zeros((2, BLK, 1, BLK), F32)], axis=2)
-        use = (row_slots[child, :, 0] == 0)[:, None, None, None]
-        sel = colsel[child, 1:][None, None, :, None]
-        head = head + jnp.where(use & (sel == 1), ahead, F32(0)) + jnp.where(use & (sel == 2), blocks, F32(0))
-    head = settled(head.reshape(2 * BLK, 4 * BLK), token)
     slabs = []
     for dx in range(4):
         for dl in range(2):
@@ -579,7 +648,7 @@
                 continue
             there = [(r, ((r // 2 - dx) % 4) * 2 + (r + dl) % 2) for r in range(8)]
             slabs.append(lax.ppermute(head, "row", there))
-    factor(1, settled(place, head[0, 0]), late)
+    factor(1, place, late)
     factor(2, place, late)
     return tuple(solve(place, source, colsel, strips, inverses, slabs, panel_rows, front, first, rest))
 

time: 332 us -> 375 us (1.13)
  Pallas kernels: 162 us -> 219 us
  starting transfers between devices: 63.5 us -> 51.6 us
  other arithmetic: 19.4 us -> 9.52 us
    pallas_call x0 -> x1, Pallas kernels: none -> 67 us  [head_rows(): pl.pallas_call(head_kernel, grid=(1,), out_shape=[jax.ShapeDtypeStruct((2...]
    ppermute x7, starting transfers between devices: 22.3 us -> 10.3 us  [local(): slabs.append(lax.ppermute(head, 'row', there))]
    ppermute x19, waiting for transfers between devices: 35.3 us -> 28.2 us  [move(): return lax.ppermute(value, BOTH, pairs)]
    ppermute x7, waiting for transfers between devices: 0.02 us -> 7.02 us  [local(): slabs.append(lax.ppermute(head, 'row', there))]
    select_n x6 -> x1, other arithmetic: 8.54 us -> 1.9 us  [gather_leading(): late = jnp.where(first, move(group[:, 2], SWAP), group[:, 3])]
    pallas_call x3, Pallas kernels: 109 us -> 103 us  [factor_strip(): pl.pallas_call(functools.partial(factor_kernel, call), out_shape=[strip,...]
    unnamed x35 -> x30, local copies, waits for them, and re-layouts: 1.38 us -> 6.16 us
    pallas_call x1, Pallas kernels: 52.5 us -> 48.4 us  [solve(): pl.pallas_call(solve_kernel, out_shape=[jax.ShapeDtypeStruct((rows, BLK),...]
  transfers between devices with their start and end apart: 29 -> 29, of which waited for: 11 -> 13; matrix products, arithmetic and copies ran while one was open for 11% -> 7% of each run, Pallas kernels for 33% -> 46%
where the time goes in v1:
time: 375 us; the launch traced here: 368 us
  Pallas kernels  219 us (58%)
  starting transfers between devices  51.6 us (14%)
  waiting for transfers between devices  44.1 us (12%)
  local copies, waits for them, and re-layouts  26.1 us (7%)
  between operations  18.6 us (5%)
  other arithmetic  9.52 us (3%)
    pallas_call x3, Pallas kernels, factor_strip(): pl.pallas_call(functools.partial(factor_kernel, call), out_shape=[strip,...  103 us
    pallas_call x1, Pallas kernels, head_rows(): pl.pallas_call(head_kernel, grid=(1,), out_shape=[jax.ShapeDtypeStruct((2...  67 us
    pallas_call x1, Pallas kernels, solve(): pl.pallas_call(solve_kernel, out_shape=[jax.ShapeDtypeStruct((rows, BLK),...  48.4 us
    ppermute x19, waiting for transfers between devices, move(): return lax.ppermute(value, BOTH, pairs)  28.2 us
    ppermute x19, starting transfers between devices, move(): return lax.ppermute(value, BOTH, pairs)  27 us
    all_to_all x2, starting transfers between devices, exchange(): lax.all_to_all(outgoing, 'row', split_axis=0, concat_axis=0, tiled=True)  14.3 us
    ppermute x7, starting transfers between devices, local(): slabs.append(lax.ppermute(head, 'row', there))  10.3 us
    all_to_all x2, waiting for transfers between devices, exchange(): lax.all_to_all(outgoing, 'row', split_axis=0, concat_axis=0, tiled=True)  8.77 us
  transfers between devices with their start and end apart: 29, of which 13 were waited for; matrix products, arithmetic and copies ran while one was open for 7% of the time, Pallas kernels for 46%

profile of v1, /device:TPU:10, one launch (start us, length us, event | category | flops | bytes accessed | tf_op | source)
XLA Modules:
  0.0 368.4 jit_solution(16723860131269863293)
XLA Ops:
  7.2 1.3 slice.234
  8.5 1.1 copy.15
  9.5 5.7 %all-to-all-start = ((f32[8,2,128,128]{3,2,1,0:T(8,128)}), f32[8,2,128,128]{3,2,1,0:T(8,128)S(1)}, u32[]{:S(2)}, u32[]{:S(2)}) async-start(f32[8,2,128,128]{3,2,1,0:T(8,128)} %bitcast.75), calls=%async_computation | async-start | bytes 2097152 | tf_op jit(solution)/shard_map/all_to_all | solution.py:609
  16.1 2.2 and_reduce_fusion.13
  18.3 1.9 fusion.9
  20.2 8.8 %all-to-all-done.f0.f1.refs_22_ = f32[8,2,128,128]{3,2,1,0:T(8,128)S(1)} async-done(((f32[8,2,128,128]{3,2,1,0:T(8,128)}), f32[8,2,128,128]{3,2,1,0:T(8,128)S(1)}, u32[]{:S(2)}, u32[]{:S(2)}) %all-to-all-start) | async-done | bytes 1048608 | tf_op jit(solution)/shard_map/all_to_all | solution.py:609
  29.2 1.2 collective-permute-done
  30.4 1.3 collective-permute-start.1
  31.7 2.3 collective-permute-start.2
  34.0 1.4 collective-permute-start.3
  36.4 4.0 %collective-permute-done.2 = f32[2,128,128]{2,1,0:T(8,128)S(1)} collective-permute-done((f32[2,128,128]{2,1,0:T(8,128)S(1)}, f32[2,128,128]{2,1,0:T(8,128)S(1)}, u32[]{:S(2)}, u32[]{:S(2)}) %collective-permute-start.2) | collective-permute-done | bytes 131104 | tf_op jit(solution)/shard_map/ppermute | solution.py:36
  41.2 2.0 collective-permute-start.4
  43.2 2.2 collective-permute-start.5
  45.4 1.8 collective-permute-start.6
  47.2 5.3 %collective-permute-done.4 = f32[4,2,128,128]{3,2,1,0:T(8,128)S(1)} collective-permute-done((f32[4,2,128,128]{3,2,1,0:T(8,128)S(1)}, f32[4,2,128,128]{3,2,1,0:T(8,128)S(1)}, u32[]{:S(2)}, u32[]{:S(2)}) %collective-permute-start.4) | collective-permute-done | bytes 524320 | tf_op jit(solution)/shard_map/ppermute | solution.py:36
  52.5 5.3 %collective-permute-done.5 = f32[4,2,128,128]{3,2,1,0:T(8,128)S(1)} collective-permute-done((f32[4,2,128,128]{3,2,1,0:T(8,128)S(1)}, f32[4,2,128,128]{3,2,1,0:T(8,128)S(1)}, u32[]{:S(2)}, u32[]{:S(2)}) %collective-permute-start.5) | collective-permute-done | bytes 524320 | tf_op jit(solution)/shard_map/ppermute | solution.py:36
  57.7 1.8 collective-permute-done.6
  59.8 1.1 slice.274.refs_0_
  61.2 1.7 collective-permute-start.8
  62.9 1.6 collective-permute-start.9
  64.5 2.0 slice.243
  66.5 3.8 %copy.14 = f32[2,8,128,384]{3,2,0,1:T(8,128)} copy(f32[2,8,128,384]{3,2,1,0:T(8,128)} %bitcast.76) | data formatting | bytes 6291456 | tf_op jit(solution)/shard_map/reshape | solution.py:606
  70.3 1.3 slice.279
  71.6 4.4 %collective-permute-done.7.refs_1_ = f32[4,2,2,128,128]{4,3,2,1,0:T(8,128)} collective-permute-done((f32[4,2,2,128,128]{4,3,2,1,0:T(8,128)}, f32[4,2,2,128,128]{4,3,2,1,0:T(8,128)}, u32[]{:S(2)}, u32[]{:S(2)}) %collective-permute-start.7) | collective-permute-done | bytes 1048608 | tf_op jit(solution)/shard_map/ppermute | solution.py:36
  76.3 8.2 %collective-permute-start.12 = (f32[4,2,2,128,128]{4,3,2,1,0:T(8,128)}, f32[4,2,2,128,128]{4,3,2,1,0:T(8,128)S(1)}, u32[]{:S(2)}, u32[]{:S(2)}) collective-permute-start(f32[4,2,2,128,128]{4,3,2,1,0:T(8,128)} %collective-permute-done.8.refs_2_), channel_id=1, source_target_pairs={{0,1},{1,0},{2,3},{3,2},{4,5},{5,4},{6,7},{7,6},{16,17},{17,16},{1... | collective-permute-start | bytes 3145736 | tf_op jit(solution)/shard_map/ppermute | solution.py:36
  84.5 4.3 %collective-permute-done.9.refs_3_ = f32[4,2,2,128,128]{4,3,2,1,0:T(8,128)} collective-permute-done((f32[4,2,2,128,128]{4,3,2,1,0:T(8,128)}, f32[4,2,2,128,128]{4,3,2,1,0:T(8,128)}, u32[]{:S(2)}, u32[]{:S(2)}) %collective-permute-start.9) | collective-permute-done | bytes 1048608 | tf_op jit(solution)/shard_map/ppermute | solution.py:36
  92.2 1.0 select_add_fusion.1
  94.7 1.0 copy-done.12
  96.8 0.9 copy-done.13
  98.9 1.0 copy-done.14
  102.4 1.9 fusion
  104.3 1.2 slice.280
  106.2 1.3 scatter.11.own
  107.5 1.4 collective-permute-start.15
  108.9 1.8 collective-permute-start.16
  111.7 1.3 scatter.10
  113.0 8.5 %all-to-all-start.1 = ((f32[8,2,128,384]{3,2,1,0:T(8,128)}), f32[8,2,128,384]{3,2,1,0:T(8,128)S(1)}, u32[]{:S(2)}, u32[]{:S(2)}) async-start(f32[8,2,128,384]{3,2,1,0:T(8,128)} %scatter.10), calls=%async_computation.1 | async-start | bytes 6291456 | tf_op jit(solution)/shard_map/all_to_all | solution.py:609
  121.5 50.9 %factor0.1 = (bf16[2048,1024]{1,0:T(8,128)(2,1)}, bf16[2048,1024]{1,0:T(8,128)(2,1)}, bf16[4,256,256]{2,1,0:T(8,128)(2,1)}, bf16[4,256,256]{2,1,0:T(8,128)(2,1)}) custom-call(s32[4]{0:T(128)} %pad_add_fusion.place, f32[4,2,2,128,128]{4,3,2,1,0:T(8,128)} %slice.274.refs_0_, f32[4,2,2,128,128]{4,3,2,1,0:T(8,128)} %collective-permute-done.7.refs_1_, ...), custom_call_target="tpu_custom_call" | custom-call | flops 71680000000 | bytes 100000000 | tf_op jit(solution)/shard_map/factor0/pallas_call | solution.py:344
  172.5 1.6 copy-done
  174.1 67.0 %head.1 = (f32[256,512]{1,0:T(8,128)}, f32[4,4,2,128,128]{4,3,2,1,0:T(8,128)}) custom-call(s32[2,2]{1,0:T(2,128)} %fusion.7.hit, s32[2,5]{1,0:T(2,128)} %compare_select_fusion.3.colsel, bf16[4,256,256]{2,1,0:T(8,128)(2,1)} %get-tuple-element.54.token.refs_6_, f32[1280,640]{1,0:T(8,128)} %refs_21_.1, f32[8,2,128,128]{3,2,1,0:T(8,128)} %copy-done.1, ...), custom_call_target="tpu_custom_call" | custom-call | tf_op jit(solution)/shard_map/head/pallas_call | solution.py:395
  242.6 4.1 %collective-permute-start.21 = (f32[256,512]{1,0:T(8,128)}, f32[256,512]{1,0:T(8,128)S(1)}, u32[]{:S(2)}, u32[]{:S(2)}) collective-permute-start(f32[256,512]{1,0:T(8,128)} %get-tuple-element.65.refs_12_), channel_id=1, source_target_pairs={{0,112},{16,96},{32,16},{48,0},{64,48},{80,32},{96,80},{112,64},{1... | collective-permute-start | bytes 1572872 | tf_op jit(solution)/shard_map/ppermute | solution.py:650
  247.0 3.3 collective-permute-start.23
  250.4 27.4 %factor1.1 = (bf16[1024,512]{1,0:T(8,128)(2,1)}, bf16[1024,512]{1,0:T(8,128)(2,1)}, bf16[2,256,256]{2,1,0:T(8,128)(2,1)}, bf16[2,256,256]{2,1,0:T(8,128)(2,1)}) custom-call(s32[4]{0:T(128)} %pad_add_fusion.place, f32[4,4,2,128,128]{4,3,2,1,0:T(8,128)} %get-tuple-element.55.refs_0_, f32[4,4,2,128,128]{4,3,2,1,0:T(8,128)} %collective-permute-done.18.refs_1_, ...), custom_call_target="tpu_custom_call" | custom-call | flops 35840000000 | bytes 100000000 | tf_op jit(solution)/shard_map/factor1/pallas_call | solution.py:344
  277.9 2.0 collective-permute-start.25
  279.9 24.9 %factor2.1 = (bf16[512,512]{1,0:T(8,128)(2,1)}, bf16[512,512]{1,0:T(8,128)(2,1)}, bf16[2,256,256]{2,1,0:T(8,128)(2,1)}, bf16[2,256,256]{2,1,0:T(8,128)(2,1)}) custom-call(s32[4]{0:T(128)} %pad_add_fusion.place, f32[4,4,2,128,128]{4,3,2,1,0:T(8,128)} %get-tuple-element.55.refs_0_, f32[4,4,2,128,128]{4,3,2,1,0:T(8,128)} %collective-permute-done.18.refs_1_, ...), custom_call_target="tpu_custom_call" | custom-call | flops 35840000000 | bytes 100000000 | tf_op jit(solution)/shard_map/factor2/pallas_call | solution.py:344
  304.8 5.6 %collective-permute-done.23.refs_17_ = f32[256,512]{1,0:T(8,128)S(1)} collective-permute-done((f32[256,512]{1,0:T(8,128)}, f32[256,512]{1,0:T(8,128)S(1)}, u32[]{:S(2)}, u32[]{:S(2)}) %collective-permute-start.23) | collective-permute-done | bytes 524320 | tf_op jit(solution)/shard_map/ppermute | solution.py:650
  311.2 1.4 collective-permute-done.25.refs_19_
  312.7 48.4 %solve.1 = (f32[1280,128]{1,0:T(8,128)}, f32[1280,640]{1,0:T(8,128)}) custom-call(s32[4]{0:T(128)} %pad_add_fusion.place, s32[2,10]{1,0:T(2,128)} %reshape.330.source, s32[2,5]{1,0:T(2,128)} %compare_select_fusion.3.colsel, bf16[2048,1024]{1,0:T(8,128)(2,1)} %get-tuple-element.52.refs_2_.refs_0_, bf16[2048,1024]{1,0:T(8,128)(2,1)} %get-tuple-element.53.refs_3_.refs_1_, ...), custom_call_target="tpu_custom_call" | custom-call | tf_op jit(solution)/shard_map/solve/pallas_call | solution.py:562
  (90 shorter events, 13.8 us)
Async XLA Ops:
  7.2 8.1 %copy-start.11 = (s32[2,64]{1,0:T(2,128)S(1)}, s32[2,64]{1,0:T(2,128)}, u32[]{:S(2)}) copy-start(s32[2,64]{1,0:T(2,128)} %param.11) | copy-start | bytes 1540
  9.5 19.4 %all-to-all-start = ((f32[8,2,128,128]{3,2,1,0:T(8,128)}), f32[8,2,128,128]{3,2,1,0:T(8,128)S(1)}, u32[]{:S(2)}, u32[]{:S(2)}) async-start(f32[8,2,128,128]{3,2,1,0:T(8,128)} %bitcast.75), calls=%async_computation | async-start | bytes 2097152 | tf_op jit(solution)/shard_map/all_to_all | solution.py:609
  15.3 297.4 %all-gather.2.cloned.1.call-start = ((), (), s32[]{:S(2)}) async-start(), calls=%async_computation.2 | async-start | bytes 8912896 | tf_op jit(solution)/shard_map/all_gather | solution.py:628
  29.0 64.3 %copy-start.1 = (f32[8,2,128,128]{3,2,1,0:T(8,128)}, f32[8,2,128,128]{3,2,1,0:T(8,128)S(1)}, u32[]{:S(2)}) copy-start(f32[8,2,128,128]{3,2,1,0:T(8,128)S(1)} %all-to-all-done.f0.f1.refs_22_) | copy-start | bytes 3145732
  29.1 1.3 collective-permute-start
  30.4 5.9 %collective-permute-start.1 = (f32[2,128,128]{2,1,0:T(8,128)S(1)}, f32[2,128,128]{2,1,0:T(8,128)S(1)}, u32[]{:S(2)}, u32[]{:S(2)}) collective-permute-start(f32[2,128,128]{2,1,0:T(8,128)S(1)} %pad_maximum_fusion.3), channel_id=1, source_target_pairs={{0,24},{1,25},{2,26},{3,27},{4,28},{5,29},{6,30},{7,31},{16,0},{17... | collective-permute-start | bytes 393224 | tf_op jit(solution)/shard_map/ppermute | solution.py:36
  31.7 8.6 %collective-permute-start.2 = (f32[2,128,128]{2,1,0:T(8,128)S(1)}, f32[2,128,128]{2,1,0:T(8,128)S(1)}, u32[]{:S(2)}, u32[]{:S(2)}) collective-permute-start(f32[2,128,128]{2,1,0:T(8,128)S(1)} %pad_maximum_fusion.3), channel_id=1, source_target_pairs={{0,8},{1,9},{2,10},{3,11},{4,12},{5,13},{6,14},{7,15},{16,24},{17,... | collective-permute-start | bytes 393224 | tf_op jit(solution)/shard_map/ppermute | solution.py:36
  34.0 7.0 %collective-permute-start.3 = (f32[2,128,128]{2,1,0:T(8,128)S(1)}, f32[2,128,128]{2,1,0:T(8,128)S(1)}, u32[]{:S(2)}, u32[]{:S(2)}) collective-permute-start(f32[2,128,128]{2,1,0:T(8,128)S(1)} %pad_maximum_fusion.3), channel_id=1, source_target_pairs={{0,16},{1,17},{2,18},{3,19},{4,20},{5,21},{6,22},{7,23},{16,8},{17... | collective-permute-start | bytes 393224 | tf_op jit(solution)/shard_map/ppermute | solution.py:36
  41.2 11.3 %collective-permute-start.4 = (f32[4,2,128,128]{3,2,1,0:T(8,128)S(1)}, f32[4,2,128,128]{3,2,1,0:T(8,128)S(1)}, u32[]{:S(2)}, u32[]{:S(2)}) collective-permute-start(f32[4,2,128,128]{3,2,1,0:T(8,128)S(1)} %get-tuple-element.92), channel_id=1, source_target_pairs={{0,2},{1,33},{2,4},{3,35},{4,6},{5,37},{6,0},{7,39},{16,18},{17,49... | collective-permute-start | bytes 1572872 | tf_op jit(solution)/shard_map/ppermute | solution.py:36
  43.2 14.6 %collective-permute-start.5 = (f32[4,2,128,128]{3,2,1,0:T(8,128)S(1)}, f32[4,2,128,128]{3,2,1,0:T(8,128)S(1)}, u32[]{:S(2)}, u32[]{:S(2)}) collective-permute-start(f32[4,2,128,128]{3,2,1,0:T(8,128)S(1)} %get-tuple-element.92), channel_id=1, source_target_pairs={{0,6},{1,97},{2,0},{3,99},{4,2},{5,101},{6,4},{7,103},{16,22},{17,... | collective-permute-start | bytes 1572872 | tf_op jit(solution)/shard_map/ppermute | solution.py:36
  45.4 14.2 %collective-permute-start.6 = (f32[4,2,128,128]{3,2,1,0:T(8,128)S(1)}, f32[4,2,128,128]{3,2,1,0:T(8,128)S(1)}, u32[]{:S(2)}, u32[]{:S(2)}) collective-permute-start(f32[4,2,128,128]{3,2,1,0:T(8,128)S(1)} %get-tuple-element.92), channel_id=1, source_target_pairs={{0,4},{1,65},{2,6},{3,67},{4,0},{5,69},{6,2},{7,71},{16,20},{17,81... | collective-permute-start | bytes 1572872 | tf_op jit(solution)/shard_map/ppermute | solution.py:36
  59.6 4.9 %copy-start.2 = (f32[2048,512]{1,0:T(8,128)S(1)}, f32[2048,512]{1,0:T(8,128)}, u32[]{:S(2)}) copy-start(f32[2048,512]{1,0:T(8,128)} %param.10) | copy-start | bytes 12582916
  60.8 15.1 %collective-permute-start.7 = (f32[4,2,2,128,128]{4,3,2,1,0:T(8,128)}, f32[4,2,2,128,128]{4,3,2,1,0:T(8,128)}, u32[]{:S(2)}, u32[]{:S(2)}) collective-permute-start(f32[4,2,2,128,128]{4,3,2,1,0:T(8,128)} %slice.274.refs_0_), channel_id=1, source_target_pairs={{0,32},{1,3},{2,34},{3,5},{4,36},{5,7},{6,38},{7,1},{16,48},{17,19... | collective-permute-start | bytes 3145736 | tf_op jit(solution)/shard_map/ppermute | solution.py:36
  61.2 15.1 %collective-permute-start.8 = (f32[4,2,2,128,128]{4,3,2,1,0:T(8,128)}, f32[4,2,2,128,128]{4,3,2,1,0:T(8,128)}, u32[]{:S(2)}, u32[]{:S(2)}) collective-permute-start(f32[4,2,2,128,128]{4,3,2,1,0:T(8,128)} %slice.274.refs_0_), channel_id=1, source_target_pairs={{0,96},{1,7},{2,98},{3,1},{4,100},{5,3},{6,102},{7,5},{16,112},{17... | collective-permute-start | bytes 3145736 | tf_op jit(solution)/shard_map/ppermute | solution.py:36
  62.9 25.9 %collective-permute-start.9 = (f32[4,2,2,128,128]{4,3,2,1,0:T(8,128)}, f32[4,2,2,128,128]{4,3,2,1,0:T(8,128)}, u32[]{:S(2)}, u32[]{:S(2)}) collective-permute-start(f32[4,2,2,128,128]{4,3,2,1,0:T(8,128)} %slice.274.refs_0_), channel_id=1, source_target_pairs={{0,64},{1,5},{2,66},{3,7},{4,68},{5,1},{6,70},{7,3},{16,80},{17,21... | collective-permute-start | bytes 3145736 | tf_op jit(solution)/shard_map/ppermute | solution.py:36
  76.0 18.8 %collective-permute-start.11 = (f32[4,2,2,128,128]{4,3,2,1,0:T(8,128)}, f32[4,2,2,128,128]{4,3,2,1,0:T(8,128)S(1)}, u32[]{:S(2)}, u32[]{:S(2)}) collective-permute-start(f32[4,2,2,128,128]{4,3,2,1,0:T(8,128)} %collective-permute-done.7.refs_1_), channel_id=1, source_target_pairs={{0,1},{1,0},{2,3},{3,2},{4,5},{5,4},{6,7},{7,6},{16,17},{17,16},{1... | collective-permute-start | bytes 3145736 | tf_op jit(solution)/shard_map/ppermute | solution.py:36
  76.3 20.5 %collective-permute-start.12 = (f32[4,2,2,128,128]{4,3,2,1,0:T(8,128)}, f32[4,2,2,128,128]{4,3,2,1,0:T(8,128)S(1)}, u32[]{:S(2)}, u32[]{:S(2)}) collective-permute-start(f32[4,2,2,128,128]{4,3,2,1,0:T(8,128)} %collective-permute-done.8.refs_2_), channel_id=1, source_target_pairs={{0,1},{1,0},{2,3},{3,2},{4,5},{5,4},{6,7},{7,6},{16,17},{17,16},{1... | collective-permute-start | bytes 3145736 | tf_op jit(solution)/shard_map/ppermute | solution.py:36
  88.8 10.0 %collective-permute-start.13 = (f32[4,2,2,128,128]{4,3,2,1,0:T(8,128)}, f32[4,2,2,128,128]{4,3,2,1,0:T(8,128)S(1)}, u32[]{:S(2)}, u32[]{:S(2)}) collective-permute-start(f32[4,2,2,128,128]{4,3,2,1,0:T(8,128)} %collective-permute-done.9.refs_3_), channel_id=1, source_target_pairs={{0,1},{1,0},{2,3},{3,2},{4,5},{5,4},{6,7},{7,6},{16,17},{17,16},{1... | collective-permute-start | bytes 3145736 | tf_op jit(solution)/shard_map/ppermute | solution.py:36
  90.2 31.3 %collective-permute-start.10 = (f32[4,2,2,128,128]{4,3,2,1,0:T(8,128)}, f32[4,2,2,128,128]{4,3,2,1,0:T(8,128)}, u32[]{:S(2)}, u32[]{:S(2)}) collective-permute-start(f32[4,2,2,128,128]{4,3,2,1,0:T(8,128)} %slice.274.refs_0_), channel_id=1, source_target_pairs={{0,1},{1,0},{2,3},{3,2},{4,5},{5,4},{6,7},{7,6},{16,17},{17,16},{1... | collective-permute-start | bytes 3145736 | tf_op jit(solution)/shard_map/ppermute | solution.py:36
  92.2 10.2 %collective-permute-start.14 = (f32[4,2,128,128]{3,2,1,0:T(8,128)}, f32[4,2,128,128]{3,2,1,0:T(8,128)}, u32[]{:S(2)}, u32[]{:S(2)}) collective-permute-start(f32[4,2,128,128]{3,2,1,0:T(8,128)} %maximum_bitcast_fusion.1), channel_id=1, source_target_pairs={{0,1},{1,0},{2,3},{3,2},{4,5},{5,4},{6,7},{7,6},{16,17},{17,16},{1... | collective-permute-start | bytes 1572872 | tf_op jit(solution)/shard_map/ppermute | solution.py:36
  94.7 1.0 copy-start.12
  96.8 1.0 copy-start.13
  98.8 1.0 copy-start.14
  101.6 0.8 copy-start.3
  107.5 65.0 %collective-permute-start.15 = (f32[4,2,128,128]{3,2,1,0:T(8,128)}, f32[4,2,128,128]{3,2,1,0:T(8,128)}, u32[]{:S(2)}, u32[]{:S(2)}) collective-permute-start(f32[4,2,128,128]{3,2,1,0:T(8,128)} %scatter.11.own), channel_id=1, source_target_pairs={{0,2},{1,3},{2,4},{3,5},{4,6},{5,7},{6,0},{7,1},{16,18},{17,19},{1... | collective-permute-start | bytes 1572872 | tf_op jit(solution)/shard_map/ppermute | solution.py:36
  108.9 63.5 %collective-permute-start.16 = (f32[4,2,128,128]{3,2,1,0:T(8,128)}, f32[4,2,128,128]{3,2,1,0:T(8,128)}, u32[]{:S(2)}, u32[]{:S(2)}) collective-permute-start(f32[4,2,128,128]{3,2,1,0:T(8,128)} %scatter.11.own), channel_id=1, source_target_pairs={{0,6},{1,7},{2,0},{3,1},{4,2},{5,3},{6,4},{7,5},{16,22},{17,23},{1... | collective-permute-start | bytes 1572872 | tf_op jit(solution)/shard_map/ppermute | solution.py:36
  110.7 61.7 %collective-permute-start.17 = (f32[4,2,128,128]{3,2,1,0:T(8,128)}, f32[4,2,128,128]{3,2,1,0:T(8,128)}, u32[]{:S(2)}, u32[]{:S(2)}) collective-permute-start(f32[4,2,128,128]{3,2,1,0:T(8,128)} %scatter.11.own), channel_id=1, source_target_pairs={{0,4},{1,5},{2,6},{3,7},{4,0},{5,1},{6,2},{7,3},{16,20},{17,21},{1... | collective-permute-start | bytes 1572872 | tf_op jit(solution)/shard_map/ppermute | solution.py:36
  113.0 59.5 %all-to-all-start.1 = ((f32[8,2,128,384]{3,2,1,0:T(8,128)}), f32[8,2,128,384]{3,2,1,0:T(8,128)S(1)}, u32[]{:S(2)}, u32[]{:S(2)}) async-start(f32[8,2,128,384]{3,2,1,0:T(8,128)} %scatter.10), calls=%async_computation.1 | async-start | bytes 6291456 | tf_op jit(solution)/shard_map/all_to_all | solution.py:609
  172.5 1.6 copy-start
  241.1 5.9 %collective-permute-start.18 = (f32[4,4,2,128,128]{4,3,2,1,0:T(8,128)}, f32[4,4,2,128,128]{4,3,2,1,0:T(8,128)}, u32[]{:S(2)}, u32[]{:S(2)}) collective-permute-start(f32[4,4,2,128,128]{4,3,2,1,0:T(8,128)} %get-tuple-element.55.refs_0_), channel_id=1, source_target_pairs={{0,1},{1,0},{2,3},{3,2},{4,5},{5,4},{6,7},{7,6},{16,17},{17,16},{1... | collective-permute-start | bytes 6291464 | tf_op jit(solution)/shard_map/ppermute | solution.py:36
  242.1 35.7 %collective-permute-start.19 = (f32[256,512]{1,0:T(8,128)}, f32[256,512]{1,0:T(8,128)S(1)}, u32[]{:S(2)}, u32[]{:S(2)}) collective-permute-start(f32[256,512]{1,0:T(8,128)} %get-tuple-element.65.refs_12_), channel_id=1, source_target_pairs={{0,16},{16,0},{32,48},{48,32},{64,80},{80,64},{96,112},{112,96},{1... | collective-permute-start | bytes 1572872 | tf_op jit(solution)/shard_map/ppermute | solution.py:650
  242.6 35.4 %collective-permute-start.20 = (f32[256,512]{1,0:T(8,128)}, f32[256,512]{1,0:T(8,128)S(1)}, u32[]{:S(2)}, u32[]{:S(2)}) collective-permute-start(f32[256,512]{1,0:T(8,128)} %get-tuple-element.65.refs_12_), channel_id=1, source_target_pairs={{0,96},{16,112},{32,0},{48,16},{64,32},{80,48},{96,64},{112,80},{1... | collective-permute-start | bytes 1572872 | tf_op jit(solution)/shard_map/ppermute | solution.py:650
  242.6 62.1 %collective-permute-start.21 = (f32[256,512]{1,0:T(8,128)}, f32[256,512]{1,0:T(8,128)S(1)}, u32[]{:S(2)}, u32[]{:S(2)}) collective-permute-start(f32[256,512]{1,0:T(8,128)} %get-tuple-element.65.refs_12_), channel_id=1, source_target_pairs={{0,112},{16,96},{32,16},{48,0},{64,48},{80,32},{96,80},{112,64},{1... | collective-permute-start | bytes 1572872 | tf_op jit(solution)/shard_map/ppermute | solution.py:650
  246.8 58.0 %collective-permute-start.22 = (f32[256,512]{1,0:T(8,128)}, f32[256,512]{1,0:T(8,128)S(1)}, u32[]{:S(2)}, u32[]{:S(2)}) collective-permute-start(f32[256,512]{1,0:T(8,128)} %get-tuple-element.65.refs_12_), channel_id=1, source_target_pairs={{0,64},{16,80},{32,96},{48,112},{64,0},{80,16},{96,32},{112,48},{1... | collective-permute-start | bytes 1572872 | tf_op jit(solution)/shard_map/ppermute | solution.py:650
  247.0 63.4 %collective-permute-start.23 = (f32[256,512]{1,0:T(8,128)}, f32[256,512]{1,0:T(8,128)S(1)}, u32[]{:S(2)}, u32[]{:S(2)}) collective-permute-start(f32[256,512]{1,0:T(8,128)} %get-tuple-element.65.refs_12_), channel_id=1, source_target_pairs={{0,80},{16,64},{32,112},{48,96},{64,16},{80,0},{96,48},{112,32},{1... | collective-permute-start | bytes 1572872 | tf_op jit(solution)/shard_map/ppermute | solution.py:650
  250.4 27.4 %copy-start.4 = (f32[256,512]{1,0:T(8,128)S(1)}, f32[256,512]{1,0:T(8,128)}, u32[]{:S(2)}) copy-start(f32[256,512]{1,0:T(8,128)} %get-tuple-element.65.refs_12_) | copy-start | bytes 1572868
  277.8 26.9 %copy-start.5 = (f32[256,512]{1,0:T(8,128)}, f32[256,512]{1,0:T(8,128)S(1)}, u32[]{:S(2)}) copy-start(f32[256,512]{1,0:T(8,128)S(1)} %collective-permute-done.19.refs_13_) | copy-start | bytes 1572868
  277.8 32.6 %collective-permute-start.24 = (f32[256,512]{1,0:T(8,128)S(1)}, f32[256,512]{1,0:T(8,128)S(1)}, u32[]{:S(2)}, u32[]{:S(2)}) collective-permute-start(f32[256,512]{1,0:T(8,128)S(1)} %copy-done.4), channel_id=1, source_target_pairs={{0,32},{16,48},{32,64},{48,80},{64,96},{80,112},{96,0},{112,16},{1... | collective-permute-start | bytes 1572872 | tf_op jit(solution)/shard_map/ppermute | solution.py:650
  277.9 26.9 %copy-start.6 = (f32[256,512]{1,0:T(8,128)}, f32[256,512]{1,0:T(8,128)S(1)}, u32[]{:S(2)}) copy-start(f32[256,512]{1,0:T(8,128)S(1)} %collective-permute-done.20.refs_14_) | copy-start | bytes 1572868
  277.9 34.7 %collective-permute-start.25 = (f32[256,512]{1,0:T(8,128)S(1)}, f32[256,512]{1,0:T(8,128)}, u32[]{:S(2)}, u32[]{:S(2)}) collective-permute-start(f32[256,512]{1,0:T(8,128)S(1)} %copy-done.4), channel_id=1, source_target_pairs={{0,48},{16,32},{32,80},{48,64},{64,112},{80,96},{96,16},{112,0},{1... | collective-permute-start | bytes 1572872 | tf_op jit(solution)/shard_map/ppermute | solution.py:650
  304.8 7.9 %copy-start.7 = (f32[256,512]{1,0:T(8,128)}, f32[256,512]{1,0:T(8,128)S(1)}, u32[]{:S(2)}) copy-start(f32[256,512]{1,0:T(8,128)S(1)} %collective-permute-done.21.refs_15_) | copy-start | bytes 1572868
  304.8 7.9 %copy-start.8 = (f32[256,512]{1,0:T(8,128)}, f32[256,512]{1,0:T(8,128)S(1)}, u32[]{:S(2)}) copy-start(f32[256,512]{1,0:T(8,128)S(1)} %collective-permute-done.22.refs_16_) | copy-start | bytes 1572868
  310.4 2.3 copy-start.9
  310.4 0.8 copy-start.10
Sparse Core Ops, SparseCore 0:
  102.5 99.8 all-gather.1
